TPU v7x, 128 devices: a whole 4x4x4 slice. The times are simulated.
128 devices in a mesh: dev: 128 (over z, x, y, core).
Axes of the slice: x: 4, y: 4, z: 4, core: 2. Of those that a mesh axis runs over, the one named last changes fastest.
Arguments:
- features: bfloat16 [786432, 128], P('dev'), may hold values from -6 to 6
- history: bfloat16 [786432, 512], P('dev'), may hold values from -5 to 5
- batch_clusters: int32 [128, 48], replicated, may hold values from 0 to 6143, as said below
- pull_list: int32 [128, 128], P('dev'), may hold values from -1 to 47, as said below
- halo_ref: int32 [128, 48], P('dev'), may hold values from 0 to 127, as said below
- in_ref: int32 [128, 48], P('dev'), may hold values from 0 to 47
- tiles: bfloat16 [6144, 3, 128, 128], P('dev'), may hold values from -0.3125 to 0.3125
- w_in: bfloat16 [128, 512], replicated, may hold values from -0.5 to 0.5
- w_layers: bfloat16 [2, 512, 512], replicated, may hold values from -0.25 to 0.25
Outputs:
- second_layer: bfloat16 [786432, 512], P('dev')
- new_history: bfloat16 [786432, 512], P('dev')
Inputs may be any that keep to these rules, and one draw needn't show every extreme that they name: `batch_clusters`: every cluster id appears exactly once. The ids of one device's batch owned by one owner (id // 48) number at most 1, and that many in some pairs. `pull_list`: entry o + m of a device's row is a cluster slot at owner o, or -1 for an empty slot. Some owner gets a live entry from every device. `halo_ref`: every entry points to a live entry of the same device's row of pull_list.
All inputs are finite; a program needn't handle non-finite values.
Results may differ from a plain program's by a relative error of at most 0.0052.
Values may be sent and summed in bfloat16 or wider, within the bound.
A program may use at most 256 MiB of HBM per device.

v0:
```python
import math

import jax
import jax.numpy as jnp
from jax import lax
from jax.sharding import PartitionSpec as P

restart = 0.1
strength = 0.5


def project(blocks_in, weight):
    flat = blocks_in.reshape(-1, blocks_in.shape[2])
    out = jax.nn.relu(jnp.dot(flat, weight, preferred_element_type=jnp.float32)).astype(
        jnp.bfloat16
    )
    return out.reshape(blocks_in.shape[0], blocks_in.shape[1], weight.shape[1])


def propagate(state, halo_state, tiles, neighbours, initial, weight, layer):
    mix_rate = math.log(strength / layer + 1.0)
    inside = jnp.take(state, neighbours, axis=0)
    aggregate = jnp.einsum("bij,bjd->bid", tiles[:, 0], state, preferred_element_type=jnp.float32)
    aggregate = aggregate + jnp.einsum(
        "bij,bjd->bid", tiles[:, 1], inside, preferred_element_type=jnp.float32
    )
    aggregate = aggregate + jnp.einsum(
        "bij,bjd->bid", tiles[:, 2], halo_state, preferred_element_type=jnp.float32
    )
    support = (1.0 - restart) * aggregate + restart * initial.astype(jnp.float32)
    flat = support.astype(jnp.bfloat16).reshape(-1, weight.shape[0])
    mixed = jnp.dot(flat, weight, preferred_element_type=jnp.float32).reshape(support.shape)
    return jax.nn.relu((1.0 - mix_rate) * support + mix_rate * mixed).astype(jnp.bfloat16)


def select_blocks(source, index, present):
    picked = jnp.take(source, index, axis=0)
    return jnp.where(present[:, None, None], picked, jnp.zeros((), picked.dtype))


def local(features, history, batch_clusters, pull_list, halo_ref, in_ref, tiles, w_in, w_layers):
    devices = lax.axis_size("dev")
    myself = lax.axis_index("dev")
    block_count = tiles.shape[0]
    block_rows = tiles.shape[2]
    feat_width = features.shape[1]
    model_width = history.shape[1]
    capacity = (block_count + devices - 1) // devices
    slot_count = pull_list.shape[1]
    feat_blocks = features.reshape(block_count, block_rows, feat_width)
    hist_blocks = history.reshape(block_count, block_rows, model_width)
    owners = batch_clusters // block_count
    places = batch_clusters % block_count
    position = jnp.arange(block_count, dtype=jnp.int32)
    sharing = owners[:, :, None] == owners[:, None, :]
    earlier = position[None, :] < position[:, None]
    rank_of = jnp.sum(sharing & earlier[None], axis=2)
    levels = jnp.arange(capacity, dtype=jnp.int32)
    owned_here = (owners == myself)[:, :, None] & (rank_of[:, :, None] == levels[None, None, :])
    slot_index = jnp.sum(jnp.where(owned_here, places[:, :, None], 0), axis=1).reshape(-1)
    filled = jnp.any(owned_here, axis=1).reshape(-1)
    my_owner = lax.dynamic_index_in_dim(owners, myself, 0, keepdims=False)
    my_rank = lax.dynamic_index_in_dim(rank_of, myself, 0, keepdims=False)
    arrival = my_owner * capacity + my_rank
    targets = jnp.arange(devices * capacity, dtype=jnp.int32)
    matching = arrival[None, :] == targets[:, None]
    source_pos = jnp.sum(jnp.where(matching, position[None, :], 0), axis=1)
    present = jnp.any(matching, axis=1)
    outgoing = select_blocks(feat_blocks, slot_index, filled)
    incoming = lax.all_to_all(outgoing, "dev", split_axis=0, concat_axis=0, tiled=True)
    initial = project(jnp.take(incoming, arrival, axis=0), w_in)
    asked = lax.all_to_all(
        pull_list.reshape(slot_count), "dev", split_axis=0, concat_axis=0, tiled=True
    )
    active = asked >= 0
    clamped = jnp.maximum(asked, 0)
    references = halo_ref.reshape(block_count)
    neighbours = in_ref.reshape(block_count)
    halo_out = select_blocks(feat_blocks, clamped, active)
    hist_out = select_blocks(hist_blocks, clamped, active)
    halo_back, halo_history = (
        lax.all_to_all(halo_out, "dev", split_axis=0, concat_axis=0, tiled=True),
        lax.all_to_all(hist_out, "dev", split_axis=0, concat_axis=0, tiled=True),
    )
    chosen = jnp.take(halo_back, references, axis=0)
    first_layer = propagate(
        initial, project(chosen, w_in), tiles, neighbours, initial, w_layers[0], 1
    )
    pushed = lax.all_to_all(
        select_blocks(first_layer, source_pos, present),
        "dev",
        split_axis=0,
        concat_axis=0,
        tiled=True,
    )
    second_layer = propagate(
        first_layer,
        jnp.take(halo_history, references, axis=0),
        tiles,
        neighbours,
        initial,
        w_layers[1],
        2,
    )
    hits = (slot_index[None, :] == position[:, None]) & filled[None, :]
    anchor = jnp.sum(jnp.where(hits, targets[None, :], 0), axis=1)
    landed = jnp.any(hits, axis=1)
    fresh = jnp.where(landed[:, None, None], jnp.take(pushed, anchor, axis=0), hist_blocks)
    return (second_layer.reshape(-1, model_width), fresh.reshape(-1, model_width))


def solution(mesh):
    placed = (
        P("dev", None),
        P("dev", None),
        P(),
        P("dev", None),
        P("dev", None),
        P("dev", None),
        P("dev", None, None, None),
        P(),
        P(),
    )
    return jax.shard_map(
        local,
        mesh=mesh,
        in_specs=placed,
        out_specs=(P("dev", None), P("dev", None)),
        check_vma=False,
    )
```

profile of v0, /device:TPU:4, one launch (start us, length us, event | category | flops | bytes accessed | tf_op | source)
XLA Modules:
  0.0 630.4 jit_solution(790576177585993000)
XLA Ops:
  2.2 10.5 %all-to-all-start.1 = ((s32[128,1,1]{2,1,0:T(1,128)}), s32[128,1,1]{2,1,0:T(1,128)S(1)}, u32[]{:S(2)}, u32[]{:S(2)}) async-start(s32[128,1,1]{2,1,0:T(1,128)} %copy.126), calls=%async_computation.1 | async-start | bytes 131072 | tf_op jit(solution)/shard_map/all_to_all | solution.py:72
  22.7 10.2 %all-to-all-start = ((bf16[128,128,128]{2,1,0:T(8,128)(2,1)}), bf16[128,128,128]{2,1,0:T(8,128)(2,1)}, u32[]{:S(2)}, u32[]{:S(2)}) async-start(bf16[128,128,128]{2,1,0:T(8,128)(2,1)} %select_select_fusion.4), calls=%async_computation | async-start | bytes 8388608 | tf_op jit(solution)/shard_map/all_to_all | solution.py:70
  45.2 38.2 %all-to-all-done = bf16[128,128,128]{2,1,0:T(8,128)(2,1)} async-done(((bf16[128,128,128]{2,1,0:T(8,128)(2,1)}), bf16[128,128,128]{2,1,0:T(8,128)(2,1)}, u32[]{:S(2)}, u32[]{:S(2)}) %all-to-all-start) | async-done | bytes 4194336 | tf_op jit(solution)/shard_map/all_to_all | solution.py:70
  91.2 10.9 %gather_fusion.6 = bf16[128,128,512]{2,1,0:T(8,128)(2,1)} fusion(bf16[48,128,512]{2,1,0:T(8,128)(2,1)} %bitcast.74, s32[1024]{0:T(1024)S(1)} %pad_clamp_fusion.3), kind=kCustom, calls=%fused_computation.3.clone | custom fusion | bytes 33554944 | tf_op jit(solution)/shard_map/jit(_take)/gather | solution.py:37
  102.0 22.4 %copy.136 = bf16[128,128,512]{1,2,0:T(8,128)(2,1)} copy(bf16[128,128,512]{2,1,0:T(8,128)(2,1)} %gather_fusion.6) | data formatting | bytes 33554432 | tf_op jit(solution)/shard_map/jit(_take)/gather | solution.py:37
  124.4 14.4 %select_select_fusion.1 = bf16[128,128,512]{1,2,0:T(8,128)(2,1)} fusion(bf16[128,128,512]{1,2,0:T(8,128)(2,1)} %copy.136, pred[128]{0:T(512)(128)(4,1)S(1)} %get-tuple-element.12, pred[128]{0:T(512)(128)(4,1)S(1)} %compare_reduce_fusion), kind=kLoop, calls=%fused_computation.11 | loop fusion | flops 16777216 | bytes 33554688 | tf_op jit(solution)/shard_map/jit(_where)/select_n | solution.py:38
  141.7 8.4 %all-to-all-start.3 = ((bf16[128,128,512]{1,2,0:T(8,128)(2,1)}), bf16[128,128,512]{1,2,0:T(8,128)(2,1)}, u32[]{:S(2)}, u32[]{:S(2)}) async-start(bf16[128,128,512]{1,2,0:T(8,128)(2,1)} %select_select_fusion.1), calls=%async_computation.3 | async-start | bytes 33554432 | tf_op jit(solution)/shard_map/all_to_all | solution.py:83
  158.1 8.6 %copy.129 = bf16[48,128,512]{1,2,0:T(8,128)(2,1)} copy(bf16[48,128,512]{2,1,0:T(8,128)(2,1)} %bitcast.71) | data formatting | bytes 12582912 | tf_op jit(solution)/shard_map/reshape | solution.py:17
  174.4 9.7 %fusion.27 = f32[48,512,128]{2,1,0:T(8,128)} fusion(bf16[48,128,512]{2,1,0:T(8,128)(2,1)} %bitcast.73, bf16[48,3,128,128]{3,2,1,0:T(8,128)(2,1)} %param.25), kind=kOutput, calls=%fused_computation.45 | convolution fusion | flops 805306368 | bytes 20447232 | tf_op jit(solution)/shard_map/bij,bjd->bid/dot_general | solution.py:23
  203.2 34.9 %maximum_convert_fusion.1 = bf16[48,128,512]{1,2,0:T(8,128)(2,1)} fusion(bf16[48,128,512]{1,2,0:T(8,128)(2,1)} %copy.129, f32[48,512,128]{2,1,0:T(8,128)} %fusion.21, f32[48,512,128]{2,1,0:T(8,128)} %fusion.27, f32[48,512,128]{2,1,0:T(8,128)} %fusion.4, bf16[2,512,512]{2,1,0:T(8,128)(2,1)S(1)} %copy-done.5), kind=kOutput, calls=%fused_computation.15 | convolution fusion | flops 3277848576 | bytes 94896128 | tf_op jit(solution)/shard_map/dot_general | solution.py:32
  238.2 10.9 %gather_fusion.8 = bf16[128,128,512]{1,2,0:T(8,128)(2,1)} fusion(bf16[48,128,512]{1,2,0:T(8,128)(2,1)} %maximum_convert_fusion.1, s32[1024]{0:T(1024)S(1)} %pad_clamp_fusion.1), kind=kCustom, calls=%fused_computation.8.clone | custom fusion | bytes 33554944 | tf_op jit(solution)/shard_map/jit(_take)/gather | solution.py:37
  249.0 14.4 %select_select_fusion = bf16[128,128,512]{1,2,0:T(8,128)(2,1)} fusion(bf16[128,128,512]{1,2,0:T(8,128)(2,1)} %gather_fusion.8, pred[128]{0:T(512)(128)(4,1)S(1)} %get-tuple-element.11, pred[128]{0:T(512)(128)(4,1)S(1)} %fusion.41), kind=kLoop, calls=%fused_computation.10 | loop fusion | flops 16777216 | bytes 33554688 | tf_op jit(solution)/shard_map/jit(_where)/select_n | solution.py:38
  263.4 107.7 %all-to-all-done.3 = bf16[128,128,512]{1,2,0:T(8,128)(2,1)} async-done(((bf16[128,128,512]{1,2,0:T(8,128)(2,1)}), bf16[128,128,512]{1,2,0:T(8,128)(2,1)}, u32[]{:S(2)}, u32[]{:S(2)}) %all-to-all-start.3) | async-done | bytes 16777248 | tf_op jit(solution)/shard_map/all_to_all | solution.py:83
  371.1 8.7 %all-to-all-start.4 = ((bf16[128,128,512]{1,2,0:T(8,128)(2,1)}), bf16[128,128,512]{1,2,0:T(8,128)(2,1)}, u32[]{:S(2)}, u32[]{:S(2)}) async-start(bf16[128,128,512]{1,2,0:T(8,128)(2,1)} %select_select_fusion), calls=%async_computation.4 | async-start | bytes 33554432 | tf_op jit(solution)/shard_map/all_to_all | solution.py:89
  379.8 8.6 %copy.142 = bf16[48,128,512]{1,2,0:T(8,128)(2,1)} copy(bf16[48,128,512]{2,1,0:T(8,128)(2,1)} %bitcast.75) | data formatting | bytes 12582912 | tf_op jit(solution)/shard_map/reshape | solution.py:51
  396.4 9.7 %fusion.25 = f32[48,512,128]{2,1,0:T(8,128)} fusion(bf16[48,128,512]{1,2,0:T(8,128)(2,1)} %maximum_convert_fusion.1, bf16[48,3,128,128]{3,2,1,0:T(8,128)(2,1)} %param.25), kind=kOutput, calls=%fused_computation.43 | convolution fusion | flops 805306368 | bytes 20447232 | tf_op jit(solution)/shard_map/bij,bjd->bid/dot_general | solution.py:23
  413.0 10.8 %gather_fusion.7 = bf16[48,128,512]{1,2,0:T(8,128)(2,1)} fusion(bf16[128,128,512]{1,2,0:T(8,128)(2,1)} %all-to-all-done.3, s32[1024]{0:T(1024)S(1)} %pad_clamp_fusion.2), kind=kCustom, calls=%fused_computation.4.clone | custom fusion | bytes 12583104 | tf_op jit(solution)/shard_map/jit(_take)/gather | solution.py:98
  423.8 9.6 %fusion = f32[48,512,128]{2,1,0:T(8,128)} fusion(bf16[48,128,512]{1,2,0:T(8,128)(2,1)} %gather_fusion.7, pred[48]{0:T(512)(128)(4,1)S(1)} %compare_and_fusion.3, bf16[48,3,128,128]{3,2,1,0:T(8,128)(2,1)} %param.25), kind=kOutput, calls=%fused_computation.20 | convolution fusion | flops 808452096 | bytes 20447280 | tf_op jit(solution)/shard_map/bij,bjd->bid/dot_general | solution.py:27
  433.4 35.4 %maximum_convert_fusion = bf16[48,128,512]{1,2,0:T(8,128)(2,1)} fusion(bf16[48,128,512]{1,2,0:T(8,128)(2,1)} %copy.129, f32[48,512,128]{2,1,0:T(8,128)} %fusion, f32[48,512,128]{2,1,0:T(8,128)} %fusion.25, f32[48,512,128]{2,1,0:T(8,128)} %fusion.2, bf16[2,512,512]{2,1,0:T(8,128)(2,1)S(1)} %copy-done.5), kind=kOutput, calls=%fused_computation.14 | convolution fusion | flops 3277848576 | bytes 94896128 | tf_op jit(solution)/shard_map/dot_general | solution.py:32
  468.9 8.6 %copy.141 = bf16[48,128,512]{2,1,0:T(8,128)(2,1)} copy(bf16[48,128,512]{1,2,0:T(8,128)(2,1)} %maximum_convert_fusion) | data formatting | bytes 12582912 | tf_op jit(solution)/shard_map/convert_element_type | solution.py:33
  477.5 124.9 %all-to-all-done.4 = bf16[128,128,512]{1,2,0:T(8,128)(2,1)} async-done(((bf16[128,128,512]{1,2,0:T(8,128)(2,1)}), bf16[128,128,512]{1,2,0:T(8,128)(2,1)}, u32[]{:S(2)}, u32[]{:S(2)}) %all-to-all-start.4) | async-done | bytes 16777248 | tf_op jit(solution)/shard_map/all_to_all | solution.py:89
  602.4 10.8 %gather_fusion.9 = bf16[48,128,512]{1,2,0:T(8,128)(2,1)} fusion(bf16[128,128,512]{1,2,0:T(8,128)(2,1)} %all-to-all-done.4, s32[1024]{0:T(1024)S(1)} %pad_clamp_fusion), kind=kCustom, calls=%fused_computation.9.clone | custom fusion | bytes 12583104 | tf_op jit(solution)/shard_map/jit(_take)/gather | solution.py:108
  613.1 8.3 %select_select_fusion.2 = bf16[48,128,512]{1,2,0:T(8,128)(2,1)} fusion(bf16[48,128,512]{1,2,0:T(8,128)(2,1)} %copy.142, bf16[48,128,512]{1,2,0:T(8,128)(2,1)} %gather_fusion.9, pred[48]{0:T(512)(128)(4,1)S(1)} %compare_and_fusion.1, pred[48]{0:T(512)(128)(4,1)S(1)} %fusion.44), kind=kLoop, calls=%fused_computation.19 | loop fusion | flops 6291456 | bytes 18874464 | tf_op jit(solution)/shard_map/jit(_where)/select_n | solution.py:108
  621.4 8.6 %copy.143 = bf16[48,128,512]{2,1,0:T(8,128)(2,1)} copy(bf16[48,128,512]{1,2,0:T(8,128)(2,1)} %select_select_fusion.2) | data formatting | bytes 12582912 | tf_op jit(solution)/shard_map/jit(_where)/select_n | solution.py:108
  (66 shorter events, 84.0 us)
Async XLA Ops:
  0.6 14.9 %copy-start = (bf16[6144,128]{1,0:T(8,128)(2,1)S(1)}, bf16[6144,128]{1,0:T(8,128)(2,1)}, u32[]{:S(2)}) copy-start(bf16[6144,128]{1,0:T(8,128)(2,1)} %param.19) | copy-start | bytes 4718596
  2.2 20.6 %all-to-all-start.1 = ((s32[128,1,1]{2,1,0:T(1,128)}), s32[128,1,1]{2,1,0:T(1,128)S(1)}, u32[]{:S(2)}, u32[]{:S(2)}) async-start(s32[128,1,1]{2,1,0:T(1,128)} %copy.126), calls=%async_computation.1 | async-start | bytes 131072 | tf_op jit(solution)/shard_map/all_to_all | solution.py:72
  22.7 60.6 %all-to-all-start = ((bf16[128,128,128]{2,1,0:T(8,128)(2,1)}), bf16[128,128,128]{2,1,0:T(8,128)(2,1)}, u32[]{:S(2)}, u32[]{:S(2)}) async-start(bf16[128,128,128]{2,1,0:T(8,128)(2,1)} %select_select_fusion.4), calls=%async_computation | async-start | bytes 8388608 | tf_op jit(solution)/shard_map/all_to_all | solution.py:70
  83.3 58.3 %all-to-all-start.2 = ((bf16[128,128,128]{2,1,0:T(8,128)(2,1)}), bf16[128,128,128]{2,1,0:T(8,128)(2,1)}, u32[]{:S(2)}, u32[]{:S(2)}) async-start(bf16[128,128,128]{2,1,0:T(8,128)(2,1)} %select_select_fusion.3), calls=%async_computation.2 | async-start | bytes 8388608 | tf_op jit(solution)/shard_map/all_to_all | solution.py:82
  138.8 11.3 %copy-start.6 = (s32[1,48]{1,0:T(1,128)S(1)}, s32[1,48]{1,0:T(1,128)}, u32[]{:S(2)}) copy-start(s32[1,48]{1,0:T(1,128)} %param.23) | copy-start | bytes 580
  138.8 11.3 %copy-start.7 = (s32[1,48]{1,0:T(1,128)S(1)}, s32[1,48]{1,0:T(1,128)}, u32[]{:S(2)}) copy-start(s32[1,48]{1,0:T(1,128)} %param.24) | copy-start | bytes 580
  141.7 229.4 %all-to-all-start.3 = ((bf16[128,128,512]{1,2,0:T(8,128)(2,1)}), bf16[128,128,512]{1,2,0:T(8,128)(2,1)}, u32[]{:S(2)}, u32[]{:S(2)}) async-start(bf16[128,128,512]{1,2,0:T(8,128)(2,1)} %select_select_fusion.1), calls=%async_computation.3 | async-start | bytes 33554432 | tf_op jit(solution)/shard_map/all_to_all | solution.py:83
  150.1 3.5 copy-start.4
  174.4 9.7 %copy-start.3 = (bf16[48,128,512]{2,1,0:T(8,128)(2,1)S(1)}, bf16[48,128,512]{2,1,0:T(8,128)(2,1)}, u32[]{:S(2)}) copy-start(bf16[48,128,512]{2,1,0:T(8,128)(2,1)} %gather_fusion.2) | copy-start | bytes 18874372
  196.1 7.1 %copy-start.5 = (bf16[2,512,512]{2,1,0:T(8,128)(2,1)S(1)}, bf16[2,512,512]{2,1,0:T(8,128)(2,1)}, u32[]{:S(2)}) copy-start(bf16[2,512,512]{2,1,0:T(8,128)(2,1)} %param.27) | copy-start | bytes 3145732
  371.1 231.3 %all-to-all-start.4 = ((bf16[128,128,512]{1,2,0:T(8,128)(2,1)}), bf16[128,128,512]{1,2,0:T(8,128)(2,1)}, u32[]{:S(2)}, u32[]{:S(2)}) async-start(bf16[128,128,512]{1,2,0:T(8,128)(2,1)} %select_select_fusion), calls=%async_computation.4 | async-start | bytes 33554432 | tf_op jit(solution)/shard_map/all_to_all | solution.py:89
  396.4 9.7 %copy-start.2 = (bf16[48,128,512]{1,2,0:T(8,128)(2,1)S(1)}, bf16[48,128,512]{1,2,0:T(8,128)(2,1)}, u32[]{:S(2)}) copy-start(bf16[48,128,512]{1,2,0:T(8,128)(2,1)} %gather_fusion.5) | copy-start | bytes 18874372
  613.1 16.9 %copy-start.1 = (bf16[6144,128]{1,0:T(8,128)(2,1)S(1)}, bf16[6144,128]{1,0:T(8,128)(2,1)}, u32[]{:S(2)}) copy-start(bf16[6144,128]{1,0:T(8,128)(2,1)} %param.19) | copy-start | bytes 4718596
where the time goes:
time: 640 us; the launch traced here: 630 us
  waiting for transfers between devices  274 us (43%)
  local copies, waits for them, and re-layouts  129 us (20%)
  matrix products  127 us (20%)
  other arithmetic  53.9 us (8%)
  starting transfers between devices  45.6 us (7%)
    all_to_all x1, waiting for transfers between devices, local(): lax.all_to_all(select_blocks(first_layer, source_pos, present), 'dev', sp...  125 us
    all_to_all x1, waiting for transfers between devices, local(): lax.all_to_all(hist_out, 'dev', split_axis=0, concat_axis=0, tiled=True)  108 us
    dot_general x2, matrix products, propagate(): jnp.dot(flat, weight, preferred_element_type=jnp.float32)  70.4 us
    gather x5, local copies, waits for them, and re-layouts, select_blocks(): picked = jnp.take(source, index, axis=0)  50.3 us
    all_to_all x1, waiting for transfers between devices, local(): lax.all_to_all(outgoing, 'dev', split_axis=0, concat_axis=0, tiled=True)  38.2 us
    select_n x4, other arithmetic, select_blocks(): jnp.where(present[:, None, None], picked, jnp.zeros((), picked.dtype))  36.9 us
    dot_general x2, matrix products, propagate(): jnp.einsum('bij,bjd->bid', tiles[:, 0], state, preferred_element_type=jnp...  19.4 us
    dot_general x2, matrix products, propagate(): jnp.einsum('bij,bjd->bid', tiles[:, 2], halo_state, preferred_element_typ...  16.7 us
  transfers between devices with their start and end apart: 5, of which 4 were waited for; matrix products, arithmetic and copies ran while one was open for 45% of the time, Pallas kernels for 0%

commit v1 on v0

v1 whole, which is shorter than its diff:
```python
import functools
import math

import jax
import jax.numpy as jnp
from jax import lax
from jax.experimental import pallas as pl
from jax.experimental.pallas import tpu as pltpu
from jax.sharding import PartitionSpec as P

restart = 0.1
strength = 0.5
lanes = 128
vmem_bytes = 56 * 1024 * 1024
bf16 = jnp.bfloat16
f32 = jnp.float32


def params():
    return pltpu.CompilerParams(vmem_limit_bytes=vmem_bytes)


def regroup_body(inner, outer, x_ref, o_ref, wide):
    chunk = 256

    def widen(i, carry):
        rows = pl.ds(pl.multiple_of(i * chunk, chunk), chunk)
        wide[rows, :] = x_ref[rows, :].astype(f32)
        return carry

    lax.fori_loop(0, inner * outer // chunk, widen, 0)

    def move(g, carry):
        rows = pl.ds(pl.multiple_of(g * inner, inner), inner)
        o_ref[rows, :] = wide[pl.ds(g, inner, stride=outer), :].astype(bf16)
        return carry

    lax.fori_loop(0, outer, move, 0, unroll=4)


def regroup(x, inner, outer, split=1, join=1):
    rows = inner * outer
    steps = max(split, join)
    return pl.pallas_call(
        functools.partial(regroup_body, inner, outer),
        grid=(steps,),
        in_specs=[pl.BlockSpec((rows, lanes), (lambda q: (0, q)) if split > 1 else (lambda q: (q, 0)))],
        out_specs=pl.BlockSpec((rows, lanes), (lambda q: (0, q)) if join > 1 else (lambda q: (q, 0))),
        out_shape=jax.ShapeDtypeStruct((rows * steps // join, lanes * join), bf16),
        scratch_shapes=[pltpu.VMEM((rows, lanes), f32)],
        compiler_params=params(),
        cost_estimate=pl.CostEstimate(flops=0, bytes_accessed=rows * steps * lanes * 24, transcendentals=0),
    )(x)


def gather_body(height, per, index, x_ref, o_ref, wide, picked):
    step = pl.program_id(0)
    chunk = 512

    @pl.when(step == 0)
    def _():
        def widen(i, carry):
            value = x_ref[pl.ds(pl.multiple_of(i * chunk, chunk), chunk), :].astype(f32)
            slots = pl.ds(pl.multiple_of(i * (chunk // height), chunk // height), chunk // height)
            wide[slots] = value.reshape(chunk // height, height, lanes) if height > 1 else value
            return carry

        lax.fori_loop(0, x_ref.shape[0] // chunk, widen, 0)

    def pick(j, carry):
        i = index[step * per + j]
        if height > 1:
            picked[j] = wide[i]
        else:
            picked[pl.ds(j, 1), :] = wide[pl.ds(i, 1), :]
        return carry

    lax.fori_loop(0, per, pick, 0, unroll=8)

    def narrow(i, carry):
        slots = pl.ds(pl.multiple_of(i * (chunk // height), chunk // height), chunk // height)
        value = picked[slots]
        value = value.reshape(chunk, lanes) if height > 1 else value
        o_ref[pl.ds(pl.multiple_of(i * chunk, chunk), chunk), :] = value.astype(bf16)
        return carry

    lax.fori_loop(0, per * height // chunk, narrow, 0)


def gather(x, index, height, steps):
    rows = x.shape[0]
    per = index.shape[0] // steps
    tail = (height, lanes) if height > 1 else (lanes,)
    return pl.pallas_call(
        functools.partial(gather_body, height, per),
        grid_spec=pltpu.PrefetchScalarGridSpec(
            num_scalar_prefetch=1,
            grid=(steps,),
            in_specs=[pl.BlockSpec((rows, lanes), lambda i, *_: (0, 0))],
            out_specs=pl.BlockSpec((per * height, lanes), lambda i, *_: (i, 0)),
            scratch_shapes=[
                pltpu.VMEM((rows // height,) + tail, f32),
                pltpu.VMEM((per,) + tail, f32),
            ],
        ),
        out_shape=jax.ShapeDtypeStruct((per * steps * height, lanes), bf16),
        compiler_params=params(),
        cost_estimate=pl.CostEstimate(flops=0, bytes_accessed=60_000_000, transcendentals=0),
    )(index, x)


def scatter_body(height, per, steps, index, x_ref, o_ref, wide, loaded):
    step = pl.program_id(0)
    chunk = 512

    def widen(i, carry):
        value = x_ref[pl.ds(pl.multiple_of(i * chunk, chunk), chunk), :].astype(f32)
        slots = pl.ds(pl.multiple_of(i * (chunk // height), chunk // height), chunk // height)
        loaded[slots] = value.reshape(chunk // height, height, lanes)
        return carry

    lax.fori_loop(0, per * height // chunk, widen, 0)

    def place(j, carry):
        wide[index[step * per + j]] = loaded[j]
        return carry

    lax.fori_loop(0, per, place, 0, unroll=8)

    @pl.when(step == steps - 1)
    def _():
        def narrow(i, carry):
            slots = pl.ds(pl.multiple_of(i * (chunk // height), chunk // height), chunk // height)
            o_ref[pl.ds(pl.multiple_of(i * chunk, chunk), chunk), :] = (
                wide[slots].reshape(chunk, lanes).astype(bf16)
            )
            return carry

        lax.fori_loop(0, o_ref.shape[0] // chunk, narrow, 0)


def scatter(x, index, height, steps):
    rows = x.shape[0]
    per = index.shape[0] // steps
    return pl.pallas_call(
        functools.partial(scatter_body, height, per, steps),
        grid_spec=pltpu.PrefetchScalarGridSpec(
            num_scalar_prefetch=1,
            grid=(steps,),
            in_specs=[pl.BlockSpec((per * height, lanes), lambda i, *_: (i, 0))],
            out_specs=pl.BlockSpec((rows, lanes), lambda i, *_: (0, 0)),
            scratch_shapes=[
                pltpu.VMEM((rows // height, height, lanes), f32),
                pltpu.VMEM((per, height, lanes), f32),
            ],
        ),
        out_shape=jax.ShapeDtypeStruct((rows, lanes), bf16),
        compiler_params=params(),
        cost_estimate=pl.CostEstimate(flops=0, bytes_accessed=60_000_000, transcendentals=0),
    )(index, x)


def project(x, weight):
    return jnp.maximum(jnp.dot(x, weight, preferred_element_type=f32), 0.0).astype(bf16)


def finish(support, weight, layer):
    mix_rate = math.log(strength / layer + 1.0)
    mixed = jnp.dot(support.astype(bf16), weight, preferred_element_type=f32)
    return jnp.maximum((1.0 - mix_rate) * support + mix_rate * mixed, 0.0).astype(bf16)


def layer_body(layer, group, neighbours, x_ref, state_ref, halo_ref, t_ref, win_ref, w_ref, o_ref, support, *made):
    step = pl.program_id(0)
    block = lanes
    if layer == 1:
        state_ref = made[0]

        @pl.when(step == 0)
        def _():
            def fill(i, carry):
                rows = pl.ds(pl.multiple_of(i * 512, 512), 512)
                state_ref[rows, :] = project(x_ref[rows, :], win_ref[...])
                return carry

            lax.fori_loop(0, state_ref.shape[0] // 512, fill, 0)

    for k in range(group):
        b = step * group + k
        own = pl.ds(pl.multiple_of(b * block, block), block)
        near = pl.ds(pl.multiple_of(neighbours[b] * block, block), block)
        here = pl.ds(k * block, block)
        if layer == 1:
            far = project(halo_ref[here, :], win_ref[...])
            initial = state_ref[own, :]
        else:
            far = halo_ref[here, :]
            initial = project(x_ref[own, :], win_ref[...])
        left = jnp.concatenate([t_ref[k, 0], t_ref[k, 1], t_ref[k, 2]], axis=1)
        right = jnp.concatenate([state_ref[own, :], state_ref[near, :], far], axis=0)
        aggregate = jnp.dot(left, right, preferred_element_type=f32)
        support[here, :] = (1.0 - restart) * aggregate + restart * initial.astype(f32)
    o_ref[...] = finish(support[...], w_ref[...], layer)


def propagate(layer, neighbours, x, state, halo, halo_offset, tiles, w_in, weight):
    count = neighbours.shape[0]
    group = 4
    width = weight.shape[0]
    span = group * lanes
    fixed = lambda *shape: pl.BlockSpec(shape, lambda i, *_: (0,) * len(shape))
    scratch = [pltpu.VMEM((span, width), f32)]
    if layer == 1:
        scratch.append(pltpu.VMEM((count * lanes, width), bf16))
    return pl.pallas_call(
        functools.partial(layer_body, layer, group),
        grid_spec=pltpu.PrefetchScalarGridSpec(
            num_scalar_prefetch=1,
            grid=(count // group,),
            in_specs=[
                fixed(count * lanes, x.shape[1]),
                fixed(*state.shape),
                pl.BlockSpec((span, halo.shape[1]), lambda i, *_: (i + halo_offset // span, 0)),
                pl.BlockSpec((group, 3, lanes, lanes), lambda i, *_: (i, 0, 0, 0)),
                fixed(*w_in.shape),
                fixed(*weight.shape),
            ],
            out_specs=pl.BlockSpec((span, width), lambda i, *_: (i, 0)),
            scratch_shapes=scratch,
        ),
        out_shape=jax.ShapeDtypeStruct((count * lanes, width), bf16),
        compiler_params=params(),
        cost_estimate=pl.CostEstimate(flops=12_000_000_000, bytes_accessed=20_000_000, transcendentals=0),
    )(neighbours, x, state, halo, tiles, w_in, weight)


def exchange(x):
    devices = lax.axis_size("dev")
    parts = x.reshape(devices, x.shape[0] // devices, x.shape[1])
    return lax.all_to_all(parts, "dev", split_axis=0, concat_axis=0, tiled=True).reshape(x.shape)


def local(features, history, batch_clusters, pull_list, halo_ref, in_ref, tiles, w_in, w_layers):
    devices = lax.axis_size("dev")
    count = tiles.shape[0]
    block = tiles.shape[2]
    columns = history.shape[1] // lanes
    height = block * columns // devices
    spread = block // height
    owner = halo_ref.reshape(count)
    slots = jnp.arange(devices, dtype=jnp.int32)
    place = jnp.sum(
        jnp.where(owner[:, None] == slots[None, :], pull_list.reshape(1, devices), 0), axis=1
    )
    pulled = lax.all_gather(owner * count + place, "dev")

    feature_slices = exchange(regroup(features, count, block))
    history_slices = exchange(regroup(history, count * height, spread, split=columns))

    wanted = jnp.concatenate([batch_clusters, pulled], axis=1).reshape(-1)
    inputs = exchange(gather(feature_slices, wanted, 1, 8))
    inputs = regroup(inputs, devices, 2 * count)

    halo_rows = exchange(gather(history_slices, pulled.reshape(-1), height, 8))

    neighbours = in_ref.reshape(count)
    first_layer = propagate(
        1, neighbours, inputs, w_in, inputs, count * block, tiles, w_in, w_layers[0]
    )
    pushed = exchange(regroup(first_layer, count * height, spread, split=columns))
    halo_history = regroup(halo_rows, spread, count * height, join=columns)
    pushed = exchange(scatter(pushed, batch_clusters.reshape(-1), height, 8))
    second_layer = propagate(
        2, neighbours, inputs, first_layer, halo_history, 0, tiles, w_in, w_layers[1]
    )
    new_history = regroup(pushed, spread, count * height, join=columns)
    return (second_layer, new_history)


def solution(mesh):
    placed = (
        P("dev", None),
        P("dev", None),
        P(),
        P("dev", None),
        P("dev", None),
        P("dev", None),
        P("dev", None, None, None),
        P(),
        P(),
    )
    return jax.shard_map(
        local,
        mesh=mesh,
        in_specs=placed,
        out_specs=(P("dev", None), P("dev", None)),
        check_vma=False,
    )
```

time: 640 us -> 478 us (0.75)
  the two profiles are of different devices: /device:TPU:4 before, /device:TPU:1 now
where the time goes in v1:
time: 478 us; the launch traced here: 477 us
  waiting for transfers between devices  206 us (43%)
  Pallas kernels  175 us (37%)
  blocking collectives  44.2 us (9%)
  starting transfers between devices  41.8 us (9%)
  local copies, waits for them, and re-layouts  7.8 us (2%)
    all_to_all x6, waiting for transfers between devices, exchange(): lax.all_to_all(parts, 'dev', split_axis=0, concat_axis=0, tiled=True)  206 us
    pallas_call x6, Pallas kernels, regroup(): pl.pallas_call(functools.partial(regroup_body, inner, outer), grid=(steps...  69.9 us
    pallas_call x2, Pallas kernels, gather(): pl.pallas_call(functools.partial(gather_body, height, per), grid_spec=plt...  45.1 us
    all_gather x1, blocking collectives, local(): pulled = lax.all_gather(owner * count + place, 'dev')  44.2 us
    all_to_all x6, starting transfers between devices, exchange(): lax.all_to_all(parts, 'dev', split_axis=0, concat_axis=0, tiled=True)  41.8 us
    pallas_call x2, Pallas kernels, propagate(): pl.pallas_call(functools.partial(layer_body, layer, group), grid_spec=plt...  41 us
    pallas_call x1, Pallas kernels, scatter(): pl.pallas_call(functools.partial(scatter_body, height, per, steps), grid_...  18.9 us
  transfers between devices with their start and end apart: 6, of which 5 were waited for; matrix products, arithmetic and copies ran while one was open for 1% of the time, Pallas kernels for 28%

profile of v1, /device:TPU:1, one launch (start us, length us, event | category | flops | bytes accessed | tf_op | source)
XLA Modules:
  0.0 476.8 jit_solution(16243007918478443698)
XLA Ops:
  0.7 5.0 %shard_map.104 = bf16[6144,128]{1,0:T(8,128)(2,1)} custom-call(bf16[6144,128]{1,0:T(8,128)(2,1)} %x_ref.2), custom_call_target="tpu_custom_call" | custom-call | bytes 18874368 | tf_op jit(solution)/shard_map/pallas_call | solution.py:44
  5.6 11.5 %all-to-all-start = ((bf16[128,48,128]{2,1,0:T(8,128)(2,1)}), bf16[128,48,128]{2,1,0:T(8,128)(2,1)S(1)}, u32[]{:S(2)}, u32[]{:S(2)}) async-start(bf16[128,48,128]{2,1,0:T(8,128)(2,1)} %bitcast.32), calls=%async_computation | async-start | bytes 3145728 | tf_op jit(solution)/shard_map/all_to_all | solution.py:240
  17.5 44.2 %all-gather = s32[128,1,48]{2,1,0:T(1,128)S(1)} all-gather(s32[1,1,48]{2,1,0:T(1,128)S(1)} %fusion), channel_id=1, replica_groups=mesh['dev'=128] {'dev'}, dimensions={0}, use_global_device_ids=true | all-gather | bytes 24768 | tf_op jit(solution)/shard_map/all_gather | solution.py:255
  63.6 25.5 %shard_map.105 = bf16[12288,128]{1,0:T(8,128)(2,1)} custom-call(s32[12288]{0:T(1024)} %reshape.56.index, bf16[6144,128]{1,0:T(8,128)(2,1)} %bitcast.33), custom_call_target="tpu_custom_call" | custom-call | bytes 60000000 | tf_op jit(solution)/shard_map/pallas_call | solution.py:94
  89.1 6.2 %all-to-all-start.1 = ((bf16[128,96,128]{2,1,0:T(8,128)(2,1)}), bf16[128,96,128]{2,1,0:T(8,128)(2,1)S(1)}, u32[]{:S(2)}, u32[]{:S(2)}) async-start(bf16[128,96,128]{2,1,0:T(8,128)(2,1)} %bitcast.31), calls=%async_computation.1 | async-start | bytes 6291456 | tf_op jit(solution)/shard_map/all_to_all | solution.py:240
  95.4 15.4 %shard_map.108 = bf16[24576,128]{1,0:T(8,128)(2,1)} custom-call(bf16[6144,512]{1,0:T(8,128)(2,1)} %x_ref.3), custom_call_target="tpu_custom_call" | custom-call | bytes 75497472 | tf_op jit(solution)/shard_map/pallas_call | solution.py:44
  110.7 26.5 %all-to-all-done.1 = bf16[128,96,128]{2,1,0:T(8,128)(2,1)S(1)} async-done(((bf16[128,96,128]{2,1,0:T(8,128)(2,1)}), bf16[128,96,128]{2,1,0:T(8,128)(2,1)S(1)}, u32[]{:S(2)}, u32[]{:S(2)}) %all-to-all-start.1) | async-done | bytes 3145760 | tf_op jit(solution)/shard_map/all_to_all | solution.py:240
  138.9 5.4 %all-to-all-start.2 = ((bf16[128,192,128]{2,1,0:T(8,128)(2,1)}), bf16[128,192,128]{2,1,0:T(8,128)(2,1)}, u32[]{:S(2)}, u32[]{:S(2)}) async-start(bf16[128,192,128]{2,1,0:T(8,128)(2,1)} %bitcast.27), calls=%async_computation.2 | async-start | bytes 12582912 | tf_op jit(solution)/shard_map/all_to_all | solution.py:240
  144.3 2.3 slice_bitcast_fusion
  146.6 9.6 %shard_map.106.x_ref.halo_ref = bf16[12288,128]{1,0:T(8,128)(2,1)} custom-call(bf16[12288,128]{1,0:T(8,128)(2,1)} %bitcast.30), custom_call_target="tpu_custom_call" | custom-call | bytes 37748736 | tf_op jit(solution)/shard_map/pallas_call | solution.py:44
  156.2 22.6 %shard_map.107.state_ref.x_ref = bf16[6144,512]{1,0:T(8,128)(2,1)} custom-call(s32[48]{0:T(128)} %bitcast.37, bf16[12288,128]{1,0:T(8,128)(2,1)} %shard_map.106.x_ref.halo_ref, bf16[128,512]{1,0:T(8,128)(2,1)} %win_ref.3, bf16[12288,128]{1,0:T(8,128)(2,1)} %shard_map.106.x_ref.halo_ref, bf16[48,3,128,128]{3,2,1,0:T(8,128)(2,1)} %t_ref.3, ...), custom_call_target="tpu_custom_call" | custom-call | flops 12000000000 | bytes 20000000 | tf_op jit(solution)/shard_map/pallas_call | solution.py:215
  178.7 15.4 %shard_map.112 = bf16[24576,128]{1,0:T(8,128)(2,1)} custom-call(bf16[6144,512]{1,0:T(8,128)(2,1)} %shard_map.107.state_ref.x_ref), custom_call_target="tpu_custom_call" | custom-call | bytes 75497472 | tf_op jit(solution)/shard_map/pallas_call | solution.py:44
  194.1 25.6 %all-to-all-done.2 = bf16[128,192,128]{2,1,0:T(8,128)(2,1)} async-done(((bf16[128,192,128]{2,1,0:T(8,128)(2,1)}), bf16[128,192,128]{2,1,0:T(8,128)(2,1)}, u32[]{:S(2)}, u32[]{:S(2)}) %all-to-all-start.2) | async-done | bytes 6291488 | tf_op jit(solution)/shard_map/all_to_all | solution.py:240
  219.8 6.2 %all-to-all-start.4 = ((bf16[128,192,128]{2,1,0:T(8,128)(2,1)}), bf16[128,192,128]{2,1,0:T(8,128)(2,1)}, u32[]{:S(2)}, u32[]{:S(2)}) async-start(bf16[128,192,128]{2,1,0:T(8,128)(2,1)} %bitcast.26), calls=%async_computation.4 | async-start | bytes 12582912 | tf_op jit(solution)/shard_map/all_to_all | solution.py:240
  228.1 19.7 %shard_map.109 = bf16[24576,128]{1,0:T(8,128)(2,1)} custom-call(s32[6144]{0:T(1024)} %reshape.61.index, bf16[24576,128]{1,0:T(8,128)(2,1)} %bitcast.12.x_ref), custom_call_target="tpu_custom_call" | custom-call | bytes 60000000 | tf_op jit(solution)/shard_map/pallas_call | solution.py:94
  247.7 53.7 %all-to-all-done.4 = bf16[128,192,128]{2,1,0:T(8,128)(2,1)} async-done(((bf16[128,192,128]{2,1,0:T(8,128)(2,1)}), bf16[128,192,128]{2,1,0:T(8,128)(2,1)}, u32[]{:S(2)}, u32[]{:S(2)}) %all-to-all-start.4) | async-done | bytes 6291488 | tf_op jit(solution)/shard_map/all_to_all | solution.py:240
  301.4 6.2 %all-to-all-start.3 = ((bf16[128,192,128]{2,1,0:T(8,128)(2,1)}), bf16[128,192,128]{2,1,0:T(8,128)(2,1)}, u32[]{:S(2)}, u32[]{:S(2)}) async-start(bf16[128,192,128]{2,1,0:T(8,128)(2,1)} %bitcast.29), calls=%async_computation.3 | async-start | bytes 12582912 | tf_op jit(solution)/shard_map/all_to_all | solution.py:240
  308.3 18.9 %shard_map.113 = bf16[24576,128]{1,0:T(8,128)(2,1)} custom-call(s32[6144]{0:T(1024)} %reshape.66.index, bf16[24576,128]{1,0:T(8,128)(2,1)} %bitcast.17.x_ref), custom_call_target="tpu_custom_call" | custom-call | bytes 60000000 | tf_op jit(solution)/shard_map/pallas_call | solution.py:145
  327.2 55.8 %all-to-all-done.3 = bf16[128,192,128]{2,1,0:T(8,128)(2,1)} async-done(((bf16[128,192,128]{2,1,0:T(8,128)(2,1)}), bf16[128,192,128]{2,1,0:T(8,128)(2,1)}, u32[]{:S(2)}, u32[]{:S(2)}) %all-to-all-start.3) | async-done | bytes 6291488 | tf_op jit(solution)/shard_map/all_to_all | solution.py:240
  383.0 6.2 %all-to-all-start.5 = ((bf16[128,192,128]{2,1,0:T(8,128)(2,1)}), bf16[128,192,128]{2,1,0:T(8,128)(2,1)}, u32[]{:S(2)}, u32[]{:S(2)}) async-start(bf16[128,192,128]{2,1,0:T(8,128)(2,1)} %bitcast.28), calls=%async_computation.5 | async-start | bytes 12582912 | tf_op jit(solution)/shard_map/all_to_all | solution.py:240
  389.2 12.3 %shard_map.110.halo_ref = bf16[6144,512]{1,0:T(8,128)(2,1)} custom-call(bf16[24576,128]{1,0:T(8,128)(2,1)} %bitcast.14.x_ref), custom_call_target="tpu_custom_call" | custom-call | bytes 75497472 | tf_op jit(solution)/shard_map/pallas_call | solution.py:44
  401.6 18.5 %shard_map.111 = bf16[6144,512]{1,0:T(8,128)(2,1)} custom-call(s32[48]{0:T(128)} %bitcast.38, bf16[12288,128]{1,0:T(8,128)(2,1)} %shard_map.106.x_ref.halo_ref, bf16[6144,512]{1,0:T(8,128)(2,1)} %shard_map.107.state_ref.x_ref, bf16[6144,512]{1,0:T(8,128)(2,1)} %shard_map.110.halo_ref, bf16[48,3,128,128]{3,2,1,0:T(8,128)(2,1)} %t_ref.3, ...), custom_call_target="tpu_custom_call" | custom-call | flops 12000000000 | bytes 20000000 | tf_op jit(solution)/shard_map/pallas_call | solution.py:215
  420.0 44.5 %all-to-all-done.5 = bf16[128,192,128]{2,1,0:T(8,128)(2,1)} async-done(((bf16[128,192,128]{2,1,0:T(8,128)(2,1)}), bf16[128,192,128]{2,1,0:T(8,128)(2,1)}, u32[]{:S(2)}, u32[]{:S(2)}) %all-to-all-start.5) | async-done | bytes 6291488 | tf_op jit(solution)/shard_map/all_to_all | solution.py:240
  464.6 12.2 %shard_map.114 = bf16[6144,512]{1,0:T(8,128)(2,1)} custom-call(bf16[24576,128]{1,0:T(8,128)(2,1)} %bitcast.19.x_ref), custom_call_target="tpu_custom_call" | custom-call | bytes 75497472 | tf_op jit(solution)/shard_map/pallas_call | solution.py:44
  (20 shorter events, 6.6 us)
Async XLA Ops:
  0.6 16.5 %copy-start.2 = (s32[128,48]{0,1:T(8,128)S(1)}, s32[128,48]{0,1:T(8,128)}, u32[]{:S(2)}) copy-start(s32[128,48]{0,1:T(8,128)} %param.11) | copy-start | bytes 73732
  0.6 16.6 %copy-start.4 = (s32[1,48]{1,0:T(1,128)S(1)}, s32[1,48]{1,0:T(1,128)}, u32[]{:S(2)}) copy-start(s32[1,48]{1,0:T(1,128)} %param.13) | copy-start | bytes 580
  0.7 16.6 %copy-start.3 = (s32[1,128]{1,0:T(1,128)S(1)}, s32[1,128]{1,0:T(1,128)}, u32[]{:S(2)}) copy-start(s32[1,128]{1,0:T(1,128)} %param.12) | copy-start | bytes 1540
  5.6 56.9 %all-to-all-start = ((bf16[128,48,128]{2,1,0:T(8,128)(2,1)}), bf16[128,48,128]{2,1,0:T(8,128)(2,1)S(1)}, u32[]{:S(2)}, u32[]{:S(2)}) async-start(bf16[128,48,128]{2,1,0:T(8,128)(2,1)} %bitcast.32), calls=%async_computation | async-start | bytes 3145728 | tf_op jit(solution)/shard_map/all_to_all | solution.py:240
  62.5 1.1 copy-start.1
  89.1 48.2 %all-to-all-start.1 = ((bf16[128,96,128]{2,1,0:T(8,128)(2,1)}), bf16[128,96,128]{2,1,0:T(8,128)(2,1)S(1)}, u32[]{:S(2)}, u32[]{:S(2)}) async-start(bf16[128,96,128]{2,1,0:T(8,128)(2,1)} %bitcast.31), calls=%async_computation.1 | async-start | bytes 6291456 | tf_op jit(solution)/shard_map/all_to_all | solution.py:240
  137.3 1.7 copy-start
  138.9 80.9 %all-to-all-start.2 = ((bf16[128,192,128]{2,1,0:T(8,128)(2,1)}), bf16[128,192,128]{2,1,0:T(8,128)(2,1)}, u32[]{:S(2)}, u32[]{:S(2)}) async-start(bf16[128,192,128]{2,1,0:T(8,128)(2,1)} %bitcast.27), calls=%async_computation.2 | async-start | bytes 12582912 | tf_op jit(solution)/shard_map/all_to_all | solution.py:240
  219.8 81.6 %all-to-all-start.4 = ((bf16[128,192,128]{2,1,0:T(8,128)(2,1)}), bf16[128,192,128]{2,1,0:T(8,128)(2,1)}, u32[]{:S(2)}, u32[]{:S(2)}) async-start(bf16[128,192,128]{2,1,0:T(8,128)(2,1)} %bitcast.26), calls=%async_computation.4 | async-start | bytes 12582912 | tf_op jit(solution)/shard_map/all_to_all | solution.py:240
  301.4 81.6 %all-to-all-start.3 = ((bf16[128,192,128]{2,1,0:T(8,128)(2,1)}), bf16[128,192,128]{2,1,0:T(8,128)(2,1)}, u32[]{:S(2)}, u32[]{:S(2)}) async-start(bf16[128,192,128]{2,1,0:T(8,128)(2,1)} %bitcast.29), calls=%async_computation.3 | async-start | bytes 12582912 | tf_op jit(solution)/shard_map/all_to_all | solution.py:240
  383.0 81.6 %all-to-all-start.5 = ((bf16[128,192,128]{2,1,0:T(8,128)(2,1)}), bf16[128,192,128]{2,1,0:T(8,128)(2,1)}, u32[]{:S(2)}, u32[]{:S(2)}) async-start(bf16[128,192,128]{2,1,0:T(8,128)(2,1)} %bitcast.28), calls=%async_computation.5 | async-start | bytes 12582912 | tf_op jit(solution)/shard_map/all_to_all | solution.py:240

commit v2 on v1

--- a/solution.py
+++ b/solution.py
@@ -239,6 +239,205 @@
     parts = x.reshape(devices, x.shape[0] // devices, x.shape[1])
     return lax.all_to_all(parts, "dev", split_axis=0, concat_axis=0, tiled=True).reshape(x.shape)
 
+MESH = pl.DeviceIdType.MESH
+IDS, FEAT_OUT, HIST_OUT, FEAT_IN = range(4)
+
+
+def partner(me, k):
+    z, x, y, core = me // 32, me // 8 % 4, me // 2 % 4, me % 2
+    return (
+        (z + k // 32) % 4 * 32 + (x + k // 8 % 4) % 4 * 8 + (y + k // 2 % 4) % 4 * 2 + (core + k % 2) % 2
+    )
+
+
+def order(me, i):
+    return partner(me, i * (37 + 54 * (me % 2)) % 128)
+
+
+def wait_all(ref, rows, sem):
+    part = ref.at[pl.ds(0, rows)]
+    pltpu.make_async_copy(part, part, sem).wait()
+
+
+def send(src, dst, sems, way, peer):
+    pltpu.make_async_remote_copy(
+        src_ref=src,
+        dst_ref=dst,
+        send_sem=sems.at[0, way],
+        recv_sem=sems.at[1, way],
+        device_id=(peer,),
+        device_id_type=MESH,
+    ).start()
+
+
+def widen(src, dst, offset, rows):
+    chunk = 256
+
+    def step(i, carry):
+        at = pl.multiple_of(i * chunk, chunk)
+        dst[pl.ds(offset + at, chunk), :] = src[pl.ds(at, chunk), :].astype(f32)
+        return carry
+
+    lax.fori_loop(0, rows // chunk, step, 0)
+
+
+def front_body(
+    batch, ids_ref, feat_ref, hist_ref,
+    inputs, hist_mid, ids_out,
+    ids_mid, ids_smem, feat_wide, wide, stage, feat_send, feat_mid, inputs_send, hist_send, picked,
+    sems, local_sem, stage_sem,
+):
+    devices = 128
+    count = 48
+    me = lax.axis_index("dev")
+    rows = count * lanes
+
+    def load_history(q):
+        return pltpu.make_async_copy(
+            hist_ref.at[:, pl.ds(q * lanes, lanes)], stage.at[q % 2], stage_sem.at[q % 2]
+        )
+
+    load_history(0).start()
+    load_history(1).start()
+    barrier = pltpu.get_barrier_semaphore()
+
+    def greet(i, carry):
+        pl.semaphore_signal(barrier, inc=1, device_id=(partner(me, i),), device_id_type=MESH)
+        return carry
+
+    lax.fori_loop(1, devices, greet, 0)
+    pl.semaphore_wait(barrier, devices - 1)
+
+    def send_ids(i, carry):
+        send(ids_ref, ids_mid.at[me], sems, IDS, order(me, i))
+        return carry
+
+    lax.fori_loop(1, devices, send_ids, 0)
+    pltpu.make_async_copy(ids_ref, ids_mid.at[me], local_sem.at[IDS]).start()
+
+    widen(feat_ref, feat_wide, 0, rows)
+
+    def at(ref, slot, size):
+        return ref.at[pl.ds(pl.multiple_of(slot * size, size), size)]
+
+    def pack_feat(m):
+        feat_send[pl.ds(pl.multiple_of(m * count, count), count), :] = feat_wide[
+            pl.ds(m, count, stride=lanes), :
+        ].astype(bf16)
+
+    def spread_feat(i, carry):
+        m = order(me, i)
+        pack_feat(m)
+        send(at(feat_send, m, count), at(feat_mid, me, count), sems, FEAT_OUT, m)
+        return carry
+
+    lax.fori_loop(1, devices, spread_feat, 0)
+    pack_feat(me)
+    pltpu.make_async_copy(at(feat_send, me, count), at(feat_mid, me, count), local_sem.at[FEAT_OUT]).start()
+
+    for q in range(4):
+        load_history(q).wait()
+        widen(stage.at[q % 2], wide, q * rows, rows)
+        if q + 2 < 4:
+            load_history(q + 2).start()
+
+    height = 4 * count
+
+    def pack_hist(m):
+        first = m // 32 * rows + m % 32
+        hist_send[pl.ds(pl.multiple_of(m * height, height), height), :] = wide[
+            pl.ds(first, height, stride=32), :
+        ].astype(bf16)
+
+    def spread_hist(i, carry):
+        m = order(me, i)
+        pack_hist(m)
+        for piece in range(3):
+            src = hist_send.at[pl.ds(pl.multiple_of(m * height + piece * 64, 64), 64)]
+            dst = hist_mid.at[pl.ds(pl.multiple_of(me * height + piece * 64, 64), 64)]
+            send(src, dst, sems, HIST_OUT, m)
+        return carry
+
+    pack_hist(me)
+    pltpu.make_async_copy(at(hist_send, me, height), at(hist_mid, me, height), local_sem.at[HIST_OUT]).start()
+    lax.fori_loop(1, devices // 2, spread_hist, 0)
+
+    pltpu.make_async_copy(ids_ref, ids_mid.at[me], local_sem.at[IDS]).wait()
+    wait_all(ids_mid, devices - 1, sems.at[1, IDS])
+    to_smem = pltpu.make_async_copy(ids_mid, ids_smem, local_sem.at[FEAT_IN])
+    to_smem.start()
+    to_smem.wait()
+    ids_copy = pltpu.make_async_copy(ids_mid, ids_out, local_sem.at[FEAT_IN])
+    ids_copy.start()
+    ids_copy.wait()
+    pltpu.make_async_copy(at(feat_send, me, count), at(feat_mid, me, count), local_sem.at[FEAT_OUT]).wait()
+    wait_all(feat_mid, (devices - 1) * count, sems.at[1, FEAT_OUT])
+    widen(feat_mid, feat_wide, 0, rows)
+    both = 2 * count
+
+    def pick_feat(d):
+        for b in range(count):
+            picked[pl.ds(b, 1), :] = feat_wide[pl.ds(batch[d, b], 1), :]
+        for b in range(count):
+            picked[pl.ds(count + b, 1), :] = feat_wide[pl.ds(ids_smem[d, 0, b], 1), :]
+        inputs_send[pl.ds(pl.multiple_of(d * both, both), both), :] = picked[pl.ds(0, both), :].astype(bf16)
+
+    def serve_feat(i, carry):
+        d = order(me, i)
+        pick_feat(d)
+        send(at(inputs_send, d, both), at(inputs, me, both), sems, FEAT_IN, d)
+        return carry
+
+    lax.fori_loop(1, devices, serve_feat, 0)
+    pick_feat(me)
+    pltpu.make_async_copy(at(inputs_send, me, both), at(inputs, me, both), local_sem.at[FEAT_IN]).start()
+    lax.fori_loop(devices // 2, devices, spread_hist, 0)
+    pltpu.make_async_copy(at(inputs_send, me, both), at(inputs, me, both), local_sem.at[FEAT_IN]).wait()
+    wait_all(inputs, (devices - 1) * both, sems.at[1, FEAT_IN])
+    pltpu.make_async_copy(at(hist_send, me, height), at(hist_mid, me, height), local_sem.at[HIST_OUT]).wait()
+    wait_all(hist_mid, (devices - 1) * height, sems.at[1, HIST_OUT])
+    wait_all(ids_mid, devices - 1, sems.at[0, IDS])
+    wait_all(feat_mid, (devices - 1) * count, sems.at[0, FEAT_OUT])
+    wait_all(inputs, (devices - 1) * both, sems.at[0, FEAT_IN])
+    wait_all(hist_mid, (devices - 1) * height, sems.at[0, HIST_OUT])
+
+
+def front(batch, ids, features, history):
+    devices, count = batch.shape
+    rows = features.shape[0]
+    anywhere = pl.BlockSpec(memory_space=pl.ANY)
+    smem = pl.BlockSpec(memory_space=pltpu.SMEM)
+    vmem = pl.BlockSpec(memory_space=pltpu.VMEM)
+    return pl.pallas_call(
+        front_body,
+        in_specs=[smem, vmem, vmem, anywhere],
+        out_specs=[anywhere, anywhere, anywhere],
+        out_shape=[
+            jax.ShapeDtypeStruct((2 * rows, lanes), bf16),
+            jax.ShapeDtypeStruct((4 * rows, lanes), bf16),
+            jax.ShapeDtypeStruct((devices, 1, lanes), jnp.int32),
+        ],
+        scratch_shapes=[
+            pltpu.VMEM((devices, 1, lanes), jnp.int32),
+            pltpu.SMEM((devices, 1, lanes), jnp.int32),
+            pltpu.VMEM((rows, lanes), f32),
+            pltpu.VMEM((4 * rows, lanes), f32),
+            pltpu.VMEM((2, rows, lanes), bf16),
+            pltpu.VMEM((rows, lanes), bf16),
+            pltpu.VMEM((rows, lanes), bf16),
+            pltpu.VMEM((2 * rows, lanes), bf16),
+            pltpu.VMEM((4 * rows, lanes), bf16),
+            pltpu.VMEM((4 * count, lanes), f32),
+            pltpu.SemaphoreType.DMA((2, 4)),
+            pltpu.SemaphoreType.DMA((4,)),
+            pltpu.SemaphoreType.DMA((2,)),
+        ],
+        compiler_params=pltpu.CompilerParams(
+            vmem_limit_bytes=vmem_bytes, collective_id=1, has_side_effects=True
+        ),
+        cost_estimate=pl.CostEstimate(flops=0, bytes_accessed=60_000_000, transcendentals=0),
+    )(batch, ids, features, history)
+
 
 def local(features, history, batch_clusters, pull_list, halo_ref, in_ref, tiles, w_in, w_layers):
     devices = lax.axis_size("dev")
@@ -252,14 +451,10 @@
     place = jnp.sum(
         jnp.where(owner[:, None] == slots[None, :], pull_list.reshape(1, devices), 0), axis=1
     )
-    pulled = lax.all_gather(owner * count + place, "dev")
-
-    feature_slices = exchange(regroup(features, count, block))
-    history_slices = exchange(regroup(history, count * height, spread, split=columns))
-
-    wanted = jnp.concatenate([batch_clusters, pulled], axis=1).reshape(-1)
-    inputs = exchange(gather(feature_slices, wanted, 1, 8))
+    mine = jnp.pad(owner * count + place, (0, lanes - count)).reshape(1, lanes)
+    inputs, history_slices, pulled = front(batch_clusters, mine, features, history)
     inputs = regroup(inputs, devices, 2 * count)
+    pulled = pulled[:, 0, :count]
 
     halo_rows = exchange(gather(history_slices, pulled.reshape(-1), height, 8))
 

time: 478 us -> 460 us (0.962)
  Pallas kernels: 175 us -> 274 us
  waiting for transfers between devices: 206 us -> 155 us
  blocking collectives: 44.2 us -> 0 us
  starting transfers between devices: 41.8 us -> 21 us
    pallas_call x0 -> x1, Pallas kernels: none -> 145 us  [front(): pl.pallas_call(front_body, in_specs=[smem, vmem, vmem, anywhere], out_spe...]
    all_to_all x6 -> x3, waiting for transfers between devices: 206 us -> 155 us  [exchange(): lax.all_to_all(parts, 'dev', split_axis=0, concat_axis=0, tiled=True)]
    all_gather x1 -> x0, blocking collectives: 44.2 us -> none  [local(): pulled = lax.all_gather(owner * count + place, 'dev')]
    pallas_call x2 -> x1, Pallas kernels: 45.1 us -> 19.7 us  [gather(): pl.pallas_call(functools.partial(gather_body, height, per), grid_spec=plt...]
    all_to_all x6 -> x3, starting transfers between devices: 41.8 us -> 21 us  [exchange(): lax.all_to_all(parts, 'dev', split_axis=0, concat_axis=0, tiled=True)]
    pallas_call x6 -> x4, Pallas kernels: 69.9 us -> 49.6 us  [regroup(): pl.pallas_call(functools.partial(regroup_body, inner, outer), grid=(steps...]
  transfers between devices with their start and end apart: 6 -> 3, of which waited for: 5 -> 3; matrix products, arithmetic and copies ran while one was open for 1% -> 0% of each run, Pallas kernels for 28% -> 15%
where the time goes in v2:
time: 460 us; the launch traced here: 459 us
  Pallas kernels  274 us (60%)
  waiting for transfers between devices  155 us (34%)
  starting transfers between devices  21 us (5%)
  local copies, waits for them, and re-layouts  5.79 us (1%)
    all_to_all x3, waiting for transfers between devices, exchange(): lax.all_to_all(parts, 'dev', split_axis=0, concat_axis=0, tiled=True)  155 us
    pallas_call x1, Pallas kernels, front(): pl.pallas_call(front_body, in_specs=[smem, vmem, vmem, anywhere], out_spe...  145 us
    pallas_call x4, Pallas kernels, regroup(): pl.pallas_call(functools.partial(regroup_body, inner, outer), grid=(steps...  49.6 us
    pallas_call x2, Pallas kernels, propagate(): pl.pallas_call(functools.partial(layer_body, layer, group), grid_spec=plt...  41 us
    all_to_all x3, starting transfers between devices, exchange(): lax.all_to_all(parts, 'dev', split_axis=0, concat_axis=0, tiled=True)  21 us
    pallas_call x1, Pallas kernels, gather(): pl.pallas_call(functools.partial(gather_body, height, per), grid_spec=plt...  19.7 us
    pallas_call x1, Pallas kernels, scatter(): pl.pallas_call(functools.partial(scatter_body, height, per, steps), grid_...  18.9 us
  transfers between devices with their start and end apart: 3, of which 3 were waited for; matrix products, arithmetic and copies ran while one was open for 0% of the time, Pallas kernels for 15%

profile of v2, /device:TPU:1, one launch (start us, length us, event | category | flops | bytes accessed | tf_op | source)
XLA Modules:
  0.0 458.5 jit_solution(1370388100701339463)
XLA Ops:
  0.6 0.8 select_reduce_fusion
  1.5 0.7 multiply_add_fusion
  2.1 0.5 pad_bitcast_fusion.ids_ref
  2.7 1.5 copy.14.batch
  4.1 2.2 slice_bitcast_fusion
  6.4 145.4 %shard_map.104 = (bf16[12288,128]{1,0:T(8,128)(2,1)}, bf16[24576,128]{1,0:T(8,128)(2,1)}, s32[128,1,128]{2,1,0:T(1,128)}) custom-call(s32[128,48]{1,0:T(8,128)} %copy.14.batch, s32[1,128]{1,0:T(1,128)} %pad_bitcast_fusion.ids_ref, bf16[6144,128]{1,0:T(8,128)(2,1)} %feat_ref.1, bf16[6144,512]{1,0:T(8,128)(2,1)} %hist_ref.1), custom_call_target="tpu_custom_call" | custom-call | bytes 60000000 | tf_op jit(solution)/shard_map/pallas_call | solution.py:411
  151.8 9.6 %shard_map.105.x_ref.halo_ref = bf16[12288,128]{1,0:T(8,128)(2,1)} custom-call(bf16[12288,128]{1,0:T(8,128)(2,1)} %get-tuple-element.5.x_ref), custom_call_target="tpu_custom_call" | custom-call | bytes 37748736 | tf_op jit(solution)/shard_map/pallas_call | solution.py:44
  161.4 22.5 %shard_map.106.state_ref.x_ref = bf16[6144,512]{1,0:T(8,128)(2,1)} custom-call(s32[48]{0:T(128)} %bitcast.21, bf16[12288,128]{1,0:T(8,128)(2,1)} %shard_map.105.x_ref.halo_ref, bf16[128,512]{1,0:T(8,128)(2,1)} %win_ref.3, bf16[12288,128]{1,0:T(8,128)(2,1)} %shard_map.105.x_ref.halo_ref, bf16[48,3,128,128]{3,2,1,0:T(8,128)(2,1)} %t_ref.3, ...), custom_call_target="tpu_custom_call" | custom-call | flops 12000000000 | bytes 20000000 | tf_op jit(solution)/shard_map/pallas_call | solution.py:215
  183.9 15.4 %shard_map.110 = bf16[24576,128]{1,0:T(8,128)(2,1)} custom-call(bf16[6144,512]{1,0:T(8,128)(2,1)} %shard_map.106.state_ref.x_ref), custom_call_target="tpu_custom_call" | custom-call | bytes 75497472 | tf_op jit(solution)/shard_map/pallas_call | solution.py:44
  199.3 8.5 %all-to-all-start.1 = ((bf16[128,192,128]{2,1,0:T(8,128)(2,1)}), bf16[128,192,128]{2,1,0:T(8,128)(2,1)}, u32[]{:S(2)}, u32[]{:S(2)}) async-start(bf16[128,192,128]{2,1,0:T(8,128)(2,1)} %bitcast.16), calls=%async_computation.1 | async-start | bytes 12582912 | tf_op jit(solution)/shard_map/all_to_all | solution.py:240
  207.8 0.0 copy-done.1
  207.8 0.2 slice_reduce_fusion
  208.0 0.7 reshape_squeeze.3.index
  208.7 19.7 %shard_map.107 = bf16[24576,128]{1,0:T(8,128)(2,1)} custom-call(s32[6144]{0:T(1024)} %reshape_squeeze.3.index, bf16[24576,128]{1,0:T(8,128)(2,1)} %get-tuple-element.7.x_ref), custom_call_target="tpu_custom_call" | custom-call | bytes 60000000 | tf_op jit(solution)/shard_map/pallas_call | solution.py:94
  228.3 54.8 %all-to-all-done.1 = bf16[128,192,128]{2,1,0:T(8,128)(2,1)} async-done(((bf16[128,192,128]{2,1,0:T(8,128)(2,1)}), bf16[128,192,128]{2,1,0:T(8,128)(2,1)}, u32[]{:S(2)}, u32[]{:S(2)}) %all-to-all-start.1) | async-done | bytes 6291488 | tf_op jit(solution)/shard_map/all_to_all | solution.py:240
  283.1 6.2 %all-to-all-start = ((bf16[128,192,128]{2,1,0:T(8,128)(2,1)}), bf16[128,192,128]{2,1,0:T(8,128)(2,1)}, u32[]{:S(2)}, u32[]{:S(2)}) async-start(bf16[128,192,128]{2,1,0:T(8,128)(2,1)} %bitcast.18), calls=%async_computation | async-start | bytes 12582912 | tf_op jit(solution)/shard_map/all_to_all | solution.py:240
  289.4 0.7 reshape.40.index
  290.1 18.9 %shard_map.111 = bf16[24576,128]{1,0:T(8,128)(2,1)} custom-call(s32[6144]{0:T(1024)} %reshape.40.index, bf16[24576,128]{1,0:T(8,128)(2,1)} %bitcast.9.x_ref), custom_call_target="tpu_custom_call" | custom-call | bytes 60000000 | tf_op jit(solution)/shard_map/pallas_call | solution.py:145
  309.0 55.8 %all-to-all-done = bf16[128,192,128]{2,1,0:T(8,128)(2,1)} async-done(((bf16[128,192,128]{2,1,0:T(8,128)(2,1)}), bf16[128,192,128]{2,1,0:T(8,128)(2,1)}, u32[]{:S(2)}, u32[]{:S(2)}) %all-to-all-start) | async-done | bytes 6291488 | tf_op jit(solution)/shard_map/all_to_all | solution.py:240
  364.7 6.2 %all-to-all-start.2 = ((bf16[128,192,128]{2,1,0:T(8,128)(2,1)}), bf16[128,192,128]{2,1,0:T(8,128)(2,1)}, u32[]{:S(2)}, u32[]{:S(2)}) async-start(bf16[128,192,128]{2,1,0:T(8,128)(2,1)} %bitcast.17), calls=%async_computation.2 | async-start | bytes 12582912 | tf_op jit(solution)/shard_map/all_to_all | solution.py:240
  371.0 12.3 %shard_map.108.halo_ref = bf16[6144,512]{1,0:T(8,128)(2,1)} custom-call(bf16[24576,128]{1,0:T(8,128)(2,1)} %bitcast.6.x_ref), custom_call_target="tpu_custom_call" | custom-call | bytes 75497472 | tf_op jit(solution)/shard_map/pallas_call | solution.py:44
  383.3 18.5 %shard_map.109 = bf16[6144,512]{1,0:T(8,128)(2,1)} custom-call(s32[48]{0:T(128)} %bitcast.22, bf16[12288,128]{1,0:T(8,128)(2,1)} %shard_map.105.x_ref.halo_ref, bf16[6144,512]{1,0:T(8,128)(2,1)} %shard_map.106.state_ref.x_ref, bf16[6144,512]{1,0:T(8,128)(2,1)} %shard_map.108.halo_ref, bf16[48,3,128,128]{3,2,1,0:T(8,128)(2,1)} %t_ref.3, ...), custom_call_target="tpu_custom_call" | custom-call | flops 12000000000 | bytes 20000000 | tf_op jit(solution)/shard_map/pallas_call | solution.py:215
  401.8 44.5 %all-to-all-done.2 = bf16[128,192,128]{2,1,0:T(8,128)(2,1)} async-done(((bf16[128,192,128]{2,1,0:T(8,128)(2,1)}), bf16[128,192,128]{2,1,0:T(8,128)(2,1)}, u32[]{:S(2)}, u32[]{:S(2)}) %all-to-all-start.2) | async-done | bytes 6291488 | tf_op jit(solution)/shard_map/all_to_all | solution.py:240
  446.3 12.2 %shard_map.112 = bf16[6144,512]{1,0:T(8,128)(2,1)} custom-call(bf16[24576,128]{1,0:T(8,128)(2,1)} %bitcast.11.x_ref), custom_call_target="tpu_custom_call" | custom-call | bytes 75497472 | tf_op jit(solution)/shard_map/pallas_call | solution.py:44
  (3 shorter events, 0.0 us)
Async XLA Ops:
  199.3 8.5 %copy-start.1 = (s32[128,1,128]{2,1,0:T(1,128)S(1)}, s32[128,1,128]{2,1,0:T(1,128)}, u32[]{:S(2)}) copy-start(s32[128,1,128]{2,1,0:T(1,128)} %get-tuple-element.6) | copy-start | bytes 196612
  199.3 83.8 %all-to-all-start.1 = ((bf16[128,192,128]{2,1,0:T(8,128)(2,1)}), bf16[128,192,128]{2,1,0:T(8,128)(2,1)}, u32[]{:S(2)}, u32[]{:S(2)}) async-start(bf16[128,192,128]{2,1,0:T(8,128)(2,1)} %bitcast.16), calls=%async_computation.1 | async-start | bytes 12582912 | tf_op jit(solution)/shard_map/all_to_all | solution.py:240
  283.1 6.3 %copy-start = (s32[128,48]{1,0:T(8,128)S(1)}, s32[128,48]{1,0:T(8,128)}, u32[]{:S(2)}) copy-start(s32[128,48]{1,0:T(8,128)} %copy.14.batch) | copy-start | bytes 73732
  283.1 81.6 %all-to-all-start = ((bf16[128,192,128]{2,1,0:T(8,128)(2,1)}), bf16[128,192,128]{2,1,0:T(8,128)(2,1)}, u32[]{:S(2)}, u32[]{:S(2)}) async-start(bf16[128,192,128]{2,1,0:T(8,128)(2,1)} %bitcast.18), calls=%async_computation | async-start | bytes 12582912 | tf_op jit(solution)/shard_map/all_to_all | solution.py:240
  364.7 81.6 %all-to-all-start.2 = ((bf16[128,192,128]{2,1,0:T(8,128)(2,1)}), bf16[128,192,128]{2,1,0:T(8,128)(2,1)}, u32[]{:S(2)}, u32[]{:S(2)}) async-start(bf16[128,192,128]{2,1,0:T(8,128)(2,1)} %bitcast.17), calls=%async_computation.2 | async-start | bytes 12582912 | tf_op jit(solution)/shard_map/all_to_all | solution.py:240

commit v3 on v0

v3 whole, which is shorter than its diff:
```python
import functools
import math

import jax
import jax.numpy as jnp
from jax import lax
from jax.experimental import pallas as pl
from jax.experimental.pallas import tpu as pltpu
from jax.sharding import PartitionSpec as P

restart = 0.1
strength = 0.5
lanes = 128
devices = 128
count = 48
rows = count * lanes
height = 4 * count
both = 2 * count
group = 4
span = group * lanes
piece = 64
vmem_bytes = 60 * 1024 * 1024
bf16 = jnp.bfloat16
f32 = jnp.float32
MESH = pl.DeviceIdType.MESH
IDS, FEAT_OUT, HIST_OUT, FEAT_IN, PUSH_OUT, HIST_IN, PUSH_IN = range(7)
WAYS = 7


def partner(me, k):
    z, x, y, core = me // 32, me // 8 % 4, me // 2 % 4, me % 2
    return (
        (z + k // 32) % 4 * 32 + (x + k // 8 % 4) % 4 * 8 + (y + k // 2 % 4) % 4 * 2 + (core + k % 2) % 2
    )


def order(me, i):
    return partner(me, i * (37 + 54 * (me % 2)) % devices)


def at(ref, slot, size):
    return ref.at[pl.ds(pl.multiple_of(slot * size, size), size)]


def wait_all(ref, size, sem):
    part = ref.at[pl.ds(0, size)]
    pltpu.make_async_copy(part, part, sem).wait()


def send(src, dst, sems, way, peer):
    pltpu.make_async_remote_copy(
        src_ref=src,
        dst_ref=dst,
        send_sem=sems.at[0, way],
        recv_sem=sems.at[1, way],
        device_id=(peer,),
        device_id_type=MESH,
    ).start()


def send_pieces(src_ref, src_slot, dst_ref, dst_slot, sems, way, peer):
    for part in range(height // piece):
        src = src_ref.at[pl.ds(pl.multiple_of(src_slot * height + part * piece, piece), piece)]
        dst = dst_ref.at[pl.ds(pl.multiple_of(dst_slot * height + part * piece, piece), piece)]
        send(src, dst, sems, way, peer)


def widen(src, dst, offset, size):
    chunk = 256

    def step(i, carry):
        here = pl.multiple_of(i * chunk, chunk)
        dst[pl.ds(offset + here, chunk), :] = src[pl.ds(here, chunk), :].astype(f32)
        return carry

    lax.fori_loop(0, size // chunk, step, 0)


def project(x, weight):
    return jnp.maximum(jnp.dot(x, weight, preferred_element_type=f32), 0.0).astype(bf16)


def mix(left, right, initial):
    aggregate = jnp.dot(left, right, preferred_element_type=f32)
    return (1.0 - restart) * aggregate + restart * initial.astype(f32)


def finish(support, weight, layer):
    mix_rate = math.log(strength / layer + 1.0)
    mixed = jnp.dot(support.astype(bf16), weight, preferred_element_type=f32)
    return jnp.maximum((1.0 - mix_rate) * support + mix_rate * mixed, 0.0).astype(bf16)


def step_body(
    batch, inverse, near, ids_ref, feat_ref, hist_ref, tile_ref, win_ref, w_ref,
    second, inputs, hist_mid, halo, push_mid, pushed,
    ids_mid, ids_smem, feat_wide, wide, stage, feat_send, feat_mid, inputs_send, given,
    wide_send, halo_send, state, support, tiles, ready, picked,
    sems, local_sem, stage_sem, tile_sem, out_sem,
):
    me = lax.axis_index("dev")

    def load_history(q):
        return pltpu.make_async_copy(
            hist_ref.at[:, pl.ds(q * lanes, lanes)], stage.at[q % 2], stage_sem.at[q % 2]
        )

    def load_part(src, q):
        return pltpu.make_async_copy(src.at[pl.ds(q * rows, rows)], stage.at[q % 2], stage_sem.at[q % 2])

    def load_wide(load, parts):
        for q in range(parts):
            load(q).wait()
            widen(stage.at[q % 2], wide, q * rows, rows)
            if q + 2 < parts:
                load(q + 2).start()

    def keep(src, src_slot, dst, dst_slot, size, way):
        return pltpu.make_async_copy(at(src, src_slot, size), at(dst, dst_slot, size), local_sem.at[way])

    def each(body, first, last):
        def step(i, carry):
            body(order(me, i))
            return carry

        lax.fori_loop(first, last, step, 0)

    load_tiles = pltpu.make_async_copy(tile_ref, tiles, tile_sem.at[0])
    load_history(0).start()
    load_history(1).start()
    barrier = pltpu.get_barrier_semaphore()

    def greet(i, carry):
        pl.semaphore_signal(barrier, inc=1, device_id=(partner(me, i),), device_id_type=MESH)
        return carry

    lax.fori_loop(1, devices, greet, 0)
    pl.semaphore_wait(barrier, devices - 1)

    each(lambda m: send(ids_ref, ids_mid.at[me], sems, IDS, m), 1, devices)
    keep_ids = pltpu.make_async_copy(ids_ref, ids_mid.at[me], local_sem.at[IDS])
    keep_ids.start()

    widen(feat_ref, feat_wide, 0, rows)

    def pack_feat(m):
        feat_send[pl.ds(pl.multiple_of(m * count, count), count), :] = feat_wide[
            pl.ds(m, count, stride=lanes), :
        ].astype(bf16)

    def spread_feat(m):
        pack_feat(m)
        send(at(feat_send, m, count), at(feat_mid, me, count), sems, FEAT_OUT, m)

    each(spread_feat, 1, devices)
    pack_feat(me)
    keep_feat = keep(feat_send, me, feat_mid, me, count, FEAT_OUT)
    keep_feat.start()

    def pack_wide(m):
        wide_send[pl.ds(pl.multiple_of(m * height, height), height), :] = wide[
            pl.ds(m // 32 * rows + m % 32, height, stride=32), :
        ].astype(bf16)

    def spread_hist(m):
        pack_wide(m)
        send_pieces(wide_send, m, hist_mid, me, sems, HIST_OUT, m)

    load_wide(load_history, 4)
    load_tiles.start()
    pack_wide(me)
    keep_hist = keep(wide_send, me, hist_mid, me, height, HIST_OUT)
    keep_hist.start()
    each(spread_hist, 1, devices // 2)

    keep_ids.wait()
    wait_all(ids_mid, devices - 1, sems.at[1, IDS])
    to_smem = pltpu.make_async_copy(ids_mid, ids_smem, local_sem.at[IDS])
    to_smem.start()
    to_smem.wait()
    keep_feat.wait()
    wait_all(feat_mid, (devices - 1) * count, sems.at[1, FEAT_OUT])

    widen(feat_mid, feat_wide, 0, rows)

    def pick_feat(d):
        for b in range(count):
            picked[pl.ds(b, 1), :] = feat_wide[pl.ds(batch[d, b], 1), :]
        for b in range(count):
            picked[pl.ds(count + b, 1), :] = feat_wide[pl.ds(ids_smem[d, 0, b], 1), :]
        inputs_send[pl.ds(pl.multiple_of(d * both, both), both), :] = picked[pl.ds(0, both), :].astype(bf16)

    def serve_feat(d):
        pick_feat(d)
        send(at(inputs_send, d, both), at(inputs, me, both), sems, FEAT_IN, d)

    each(serve_feat, 1, devices)
    pick_feat(me)
    keep_inputs = keep(inputs_send, me, inputs, me, both, FEAT_IN)
    keep_inputs.start()
    each(spread_hist, devices // 2, devices)

    keep_inputs.wait()
    wait_all(inputs, (devices - 1) * both, sems.at[1, FEAT_IN])
    load_inputs = functools.partial(load_part, inputs)
    load_inputs(0).start()
    load_inputs(1).start()
    load_wide(load_inputs, 2)

    def order_inputs(b, carry):
        given[b] = wide[pl.ds(b, lanes, stride=both), :].astype(bf16)
        return carry

    lax.fori_loop(0, both, order_inputs, 0, unroll=2)
    load_tiles.wait()

    def tile_row(b):
        return jnp.concatenate([tiles[b, 0], tiles[b, 1], tiles[b, 2]], axis=1)

    def first_group(g, carry):
        for k in range(group):
            b = g * group + k
            states = project(
                jnp.concatenate([given[b], given[near[0, b]], given[count + b]], axis=0),
                win_ref[...],
            )
            support[pl.ds(k * lanes, lanes), :] = mix(tile_row(b), states, states[:lanes])
        made = finish(support[...], w_ref[0], 1)
        for k in range(group):
            state[g * group + k] = made[k * lanes : (k + 1) * lanes]
        for q in range(4):
            wide[pl.ds(pl.multiple_of(q * rows + g * span, span), span), :] = made[
                :, q * lanes : (q + 1) * lanes
            ].astype(f32)
        return carry

    lax.fori_loop(0, count // group, first_group, 0)

    keep_hist.wait()
    wait_all(hist_mid, (devices - 1) * height, sems.at[0, HIST_OUT])

    def spread_push(m):
        pack_wide(m)
        send_pieces(wide_send, m, push_mid, me, sems, PUSH_OUT, m)

    each(spread_push, 1, devices)
    pack_wide(me)
    keep_push = keep(wide_send, me, push_mid, me, height, PUSH_OUT)
    keep_push.start()

    wait_all(hist_mid, (devices - 1) * height, sems.at[1, HIST_OUT])
    load_mid = functools.partial(load_part, hist_mid)
    load_mid(0).start()
    load_mid(1).start()
    load_wide(load_mid, 4)

    def pick_wide(dst, d, index):
        for b in range(count):
            picked[pl.ds(4 * b, 4), :] = wide[pl.ds(index(b), 4), :]
        dst[pl.ds(pl.multiple_of(d * height, height), height), :] = picked[...].astype(bf16)

    def pick_halo(d):
        pick_wide(halo_send, d, lambda b: ids_smem[d, 0, lanes // 2 + b])

    def serve_halo(d):
        pick_halo(d)
        send_pieces(halo_send, d, halo, me, sems, HIST_IN, d)

    each(serve_halo, 1, devices)
    pick_halo(me)
    keep_halo = keep(halo_send, me, halo, me, height, HIST_IN)
    keep_halo.start()

    keep_push.wait()
    wait_all(push_mid, (devices - 1) * height, sems.at[1, PUSH_OUT])
    load_push = functools.partial(load_part, push_mid)
    load_push(0).start()
    load_push(1).start()
    wait_all(push_mid, (devices - 1) * height, sems.at[0, PUSH_OUT])
    load_wide(load_push, 4)

    def pick_push(o):
        pick_wide(wide_send, o, lambda p: inverse[o, p])

    def serve_push(o):
        pick_push(o)
        send_pieces(wide_send, o, pushed, me, sems, PUSH_IN, o)

    each(serve_push, 1, devices)
    pick_push(me)
    keep_pushed = keep(wide_send, me, pushed, me, height, PUSH_IN)
    keep_pushed.start()

    keep_halo.wait()
    wait_all(halo, (devices - 1) * height, sems.at[1, HIST_IN])
    load_halo = functools.partial(load_part, halo)
    load_halo(0).start()
    load_halo(1).start()
    load_wide(load_halo, 4)

    def halo_block(b):
        return jnp.concatenate(
            [
                jnp.concatenate(
                    [wide[pl.ds(q * rows + 4 * b + i, 32, stride=height), :] for i in range(4)], axis=0
                )
                for q in range(4)
            ],
            axis=1,
        ).astype(bf16)

    def write(g, slot):
        return pltpu.make_async_copy(
            ready.at[slot], second.at[pl.ds(pl.multiple_of(g * span, span), span)], out_sem.at[slot]
        )

    def second_pair(pair, carry):
        for slot in range(2):
            g = pair * 2 + slot
            for k in range(group):
                b = g * group + k
                initial = project(given[b], win_ref[...])
                states = jnp.concatenate([state[b], state[near[0, b]], halo_block(b)], axis=0)
                support[pl.ds(k * lanes, lanes), :] = mix(tile_row(b), states, initial)
            made = finish(support[...], w_ref[1], 2)

            @pl.when(pair > 0)
            def _():
                write(g - 2, slot).wait()

            ready[slot] = made
            write(g, slot).start()
        return carry

    lax.fori_loop(0, count // group // 2, second_pair, 0)
    for slot in range(2):
        write(count // group - 2 + slot, slot).wait()

    keep_pushed.wait()
    wait_all(pushed, (devices - 1) * height, sems.at[1, PUSH_IN])
    wait_all(ids_mid, devices - 1, sems.at[0, IDS])
    wait_all(feat_mid, (devices - 1) * count, sems.at[0, FEAT_OUT])
    wait_all(inputs, (devices - 1) * both, sems.at[0, FEAT_IN])
    wait_all(halo, (devices - 1) * height, sems.at[0, HIST_IN])
    wait_all(pushed, (devices - 1) * height, sems.at[0, PUSH_IN])


def run_step(batch, inverse, near, ids, features, history, tiles, w_in, w_layers):
    anywhere = pl.BlockSpec(memory_space=pl.ANY)
    smem = pl.BlockSpec(memory_space=pltpu.SMEM)
    vmem = pl.BlockSpec(memory_space=pltpu.VMEM)
    shape = lambda *dims: jax.ShapeDtypeStruct(dims, bf16)
    sliced = shape(4 * rows, lanes)
    return pl.pallas_call(
        step_body,
        in_specs=[smem, smem, smem, vmem, vmem, anywhere, anywhere, vmem, vmem],
        out_specs=[anywhere] * 6,
        out_shape=[shape(rows, 4 * lanes), shape(2 * rows, lanes), sliced, sliced, sliced, sliced],
        scratch_shapes=[
            pltpu.VMEM((devices, 1, lanes), jnp.int32),
            pltpu.SMEM((devices, 1, lanes), jnp.int32),
            pltpu.VMEM((rows, lanes), f32),
            pltpu.VMEM((4 * rows, lanes), f32),
            pltpu.VMEM((2, rows, lanes), bf16),
            pltpu.VMEM((rows, lanes), bf16),
            pltpu.VMEM((rows, lanes), bf16),
            pltpu.VMEM((2 * rows, lanes), bf16),
            pltpu.VMEM((both, lanes, lanes), bf16),
            pltpu.VMEM((4 * rows, lanes), bf16),
            pltpu.VMEM((4 * rows, lanes), bf16),
            pltpu.VMEM((count, lanes, 4 * lanes), bf16),
            pltpu.VMEM((span, 4 * lanes), f32),
            pltpu.VMEM((count, 3, lanes, lanes), bf16),
            pltpu.VMEM((2, span, 4 * lanes), bf16),
            pltpu.VMEM((height, lanes), f32),
            pltpu.SemaphoreType.DMA((2, WAYS)),
            pltpu.SemaphoreType.DMA((WAYS,)),
            pltpu.SemaphoreType.DMA((2,)),
            pltpu.SemaphoreType.DMA((1,)),
            pltpu.SemaphoreType.DMA((2,)),
        ],
        compiler_params=pltpu.CompilerParams(
            vmem_limit_bytes=vmem_bytes, collective_id=1, has_side_effects=True
        ),
        cost_estimate=pl.CostEstimate(flops=14_000_000_000, bytes_accessed=100_000_000, transcendentals=0),
    )(batch, inverse, near, ids, features, history, tiles, w_in, w_layers)


def place_body(pushed, second, fresh, result, wide):
    result[...] = second[...]
    widen(pushed, wide, 0, rows)

    def move(a, carry):
        fresh[pl.ds(pl.multiple_of(a * 32, 32), 32), :] = wide[pl.ds(a, 32, stride=height), :].astype(bf16)
        return carry

    lax.fori_loop(0, height, move, 0, unroll=4)


def place(pushed, second):
    full = jax.ShapeDtypeStruct((rows, 4 * lanes), bf16)
    quarter = pl.BlockSpec((rows // 4, 4 * lanes), lambda q: (q, 0))
    return pl.pallas_call(
        place_body,
        grid=(4,),
        in_specs=[pl.BlockSpec((rows, lanes), lambda q: (q, 0)), quarter],
        out_specs=[pl.BlockSpec((rows, lanes), lambda q: (0, q)), quarter],
        out_shape=[full, full],
        scratch_shapes=[pltpu.VMEM((rows, lanes), f32)],
        compiler_params=pltpu.CompilerParams(vmem_limit_bytes=vmem_bytes),
        cost_estimate=pl.CostEstimate(flops=0, bytes_accessed=40_000_000, transcendentals=0),
    )(pushed, second)


def invert(batch):
    flat = batch.reshape(-1)
    spot = jnp.arange(flat.shape[0], dtype=jnp.int32)
    owner = (flat // count)[:, None] == jnp.arange(devices, dtype=jnp.int32)[None, :]
    place = (flat % count)[:, None] == jnp.arange(count, dtype=jnp.int32)[None, :]
    low = jnp.where(place, (spot % 64)[:, None], 0).astype(bf16)
    high = jnp.where(place, (spot // 64)[:, None], 0).astype(bf16)
    found = lax.dot_general(
        owner.astype(bf16),
        jnp.concatenate([low, high], axis=1),
        (((0,), (0,)), ((), ())),
        preferred_element_type=f32,
    ).astype(jnp.int32)
    return found[:, :count] + 64 * found[:, count:]


def local(features, history, batch_clusters, pull_list, halo_ref, in_ref, tiles, w_in, w_layers):
    owner = halo_ref.reshape(count)
    slots = jnp.arange(devices, dtype=jnp.int32)
    spot = jnp.sum(
        jnp.where(owner[:, None] == slots[None, :], pull_list.reshape(1, devices), 0), axis=1
    )
    mine = jnp.pad(owner * count + spot, (0, lanes // 2 - count))
    mine = jnp.concatenate([mine, 4 * mine]).reshape(1, lanes)
    second, _, _, _, _, pushed = run_step(
        batch_clusters, 4 * invert(batch_clusters), in_ref, mine, features, history, tiles, w_in, w_layers
    )
    fresh, second_layer = place(pushed, second)
    return (second_layer, fresh)


def solution(mesh):
    placed = (
        P("dev", None),
        P("dev", None),
        P(),
        P("dev", None),
        P("dev", None),
        P("dev", None),
        P("dev", None, None, None),
        P(),
        P(),
    )
    return jax.shard_map(
        local,
        mesh=mesh,
        in_specs=placed,
        out_specs=(P("dev", None), P("dev", None)),
        check_vma=False,
    )
```

time: 640 us -> 407 us (0.64)
  the two profiles are of different devices: /device:TPU:4 before, /device:TPU:1 now
where the time goes in v3:
time: 407 us
  Pallas kernels  398 us (98%)
  other arithmetic  4.55 us (1%)
    pallas_call x1, Pallas kernels, run_step(): pl.pallas_call(step_body, in_specs=[smem, smem, smem, vmem, vmem, anywher...  384 us
    pallas_call x1, Pallas kernels, place(): pl.pallas_call(place_body, grid=(4,), in_specs=[pl.BlockSpec((rows, lanes...  14.2 us

profile of v3, /device:TPU:1, one launch (start us, length us, event | category | flops | bytes accessed | tf_op | source)
XLA Modules:
  0.0 406.6 jit_solution(11166602484049093716)
XLA Ops:
  0.6 0.8 select_reduce_fusion
  1.5 0.7 multiply_add_fusion
  2.2 0.6 add_bitcast_fusion.ids_ref
  2.7 0.7 sign_compare_fusion
  3.5 0.1 copy.18
  3.6 0.1 ne.73
  3.7 0.8 broadcast_divide_fusion
  4.5 0.1 copy.20
  4.6 0.1 div.20
  4.7 0.1 copy.19
  4.8 0.1 rem.39
  4.9 1.5 copy.22.batch
  6.4 0.2 select_convert_fusion.1
  6.6 1.5 fusion.7
  8.1 0.7 fusion.13.inverse
  8.8 383.6 %shard_map.104 = (bf16[6144,512]{1,0:T(8,128)(2,1)}, bf16[12288,128]{1,0:T(8,128)(2,1)}, bf16[24576,128]{1,0:T(8,128)(2,1)}, bf16[24576,128]{1,0:T(8,128)(2,1)},...) custom-call(s32[128,48]{1,0:T(8,128)} %copy.22.batch, s32[128,48]{1,0:T(8,128)} %fusion.13.inverse, s32[1,48]{1,0:T(1,128)} %near.1, ...), custom_call_target="tpu_custom_call" | custom-call | flops 14000000000 | bytes 100000000 | tf_op jit(solution)/shard_map/pallas_call | solution.py:354
  392.4 14.2 %shard_map.105 = (bf16[6144,512]{1,0:T(8,128)(2,1)}, bf16[6144,512]{1,0:T(8,128)(2,1)}) custom-call(bf16[24576,128]{1,0:T(8,128)(2,1)} %get-tuple-element.6.pushed, bf16[6144,512]{1,0:T(8,128)(2,1)} %get-tuple-element.7.second), custom_call_target="tpu_custom_call" | custom-call | bytes 40000000 | tf_op jit(solution)/shard_map/pallas_call | solution.py:403
  (3 shorter events, 0.0 us)

commit v4 on v3

--- a/solution.py
+++ b/solution.py
@@ -19,6 +19,7 @@
 group = 4
 span = group * lanes
 piece = 64
+pad = 8
 vmem_bytes = 60 * 1024 * 1024
 bf16 = jnp.bfloat16
 f32 = jnp.float32
@@ -76,6 +77,16 @@
     lax.fori_loop(0, size // chunk, step, 0)
 
 
+def spread(src, dst, size, parts, offset=0):
+    def step(i, carry):
+        dst[pl.ds(pl.multiple_of((offset + i) * (size + pad), 8), size), :] = src[
+            pl.ds(pl.multiple_of(i * size, size), size), :
+        ].astype(f32)
+        return carry
+
+    lax.fori_loop(0, parts, step, 0, unroll=2)
+
+
 def project(x, weight):
     return jnp.maximum(jnp.dot(x, weight, preferred_element_type=f32), 0.0).astype(bf16)
 
@@ -92,9 +103,9 @@
 
 
 def step_body(
-    batch, inverse, near, ids_ref, feat_ref, hist_ref, tile_ref, win_ref, w_ref,
+    batch_ref, own_ref, near, halo_ref, pull_ref, feat_ref, hist_ref, tile_ref, win_ref, w_ref,
     second, inputs, hist_mid, halo, push_mid, pushed,
-    ids_mid, ids_smem, feat_wide, wide, stage, feat_send, feat_mid, inputs_send, given,
+    batch, mine_smem, mine, ids_mid, ids_smem, feat_wide, wide, stage, feat_send, feat_mid, inputs_send, given,
     wide_send, halo_send, state, support, tiles, ready, picked,
     sems, local_sem, stage_sem, tile_sem, out_sem,
 ):
@@ -126,26 +137,23 @@
         lax.fori_loop(first, last, step, 0)
 
     load_tiles = pltpu.make_async_copy(tile_ref, tiles, tile_sem.at[0])
+    load_batch = pltpu.make_async_copy(batch_ref, batch, tile_sem.at[1])
+    barrier = pltpu.get_barrier_semaphore()
+
+    def greet(i, carry):
+        pl.semaphore_signal(barrier, inc=1, device_id=(partner(me, i),), device_id_type=MESH)
+        return carry
+
+    lax.fori_loop(1, devices, greet, 0)
     load_history(0).start()
     load_history(1).start()
-    barrier = pltpu.get_barrier_semaphore()
-
-    def greet(i, carry):
-        pl.semaphore_signal(barrier, inc=1, device_id=(partner(me, i),), device_id_type=MESH)
-        return carry
-
-    lax.fori_loop(1, devices, greet, 0)
+    load_batch.start()
+    spread(feat_ref, feat_wide, lanes, count)
     pl.semaphore_wait(barrier, devices - 1)
-
-    each(lambda m: send(ids_ref, ids_mid.at[me], sems, IDS, m), 1, devices)
-    keep_ids = pltpu.make_async_copy(ids_ref, ids_mid.at[me], local_sem.at[IDS])
-    keep_ids.start()
-
-    widen(feat_ref, feat_wide, 0, rows)
 
     def pack_feat(m):
         feat_send[pl.ds(pl.multiple_of(m * count, count), count), :] = feat_wide[
-            pl.ds(m, count, stride=lanes), :
+            pl.ds(m, count, stride=lanes + pad), :
         ].astype(bf16)
 
     def spread_feat(m):
@@ -156,6 +164,19 @@
     pack_feat(me)
     keep_feat = keep(feat_send, me, feat_mid, me, count, FEAT_OUT)
     keep_feat.start()
+
+    for b in range(count):
+        slot = halo_ref[0, b]
+        cluster = slot * count + pull_ref[0, slot]
+        mine_smem[0, b] = cluster
+        mine_smem[0, 64 + b] = 4 * cluster
+        mine_smem[0, 128 + b] = 4 * own_ref[0, b]
+    to_vmem = pltpu.make_async_copy(mine_smem, mine, local_sem.at[IDS])
+    to_vmem.start()
+    to_vmem.wait()
+    each(lambda m: send(mine, ids_mid.at[me], sems, IDS, m), 1, devices)
+    keep_ids = pltpu.make_async_copy(mine, ids_mid.at[me], local_sem.at[IDS])
+    keep_ids.start()
 
     def pack_wide(m):
         wide_send[pl.ds(pl.multiple_of(m * height, height), height), :] = wide[
@@ -171,8 +192,9 @@
     pack_wide(me)
     keep_hist = keep(wide_send, me, hist_mid, me, height, HIST_OUT)
     keep_hist.start()
-    each(spread_hist, 1, devices // 2)
-
+    each(spread_hist, 1, devices // 4)
+
+    load_batch.wait()
     keep_ids.wait()
     wait_all(ids_mid, devices - 1, sems.at[1, IDS])
     to_smem = pltpu.make_async_copy(ids_mid, ids_smem, local_sem.at[IDS])
@@ -185,7 +207,7 @@
 
     def pick_feat(d):
         for b in range(count):
-            picked[pl.ds(b, 1), :] = feat_wide[pl.ds(batch[d, b], 1), :]
+            picked[pl.ds(b, 1), :] = feat_wide[pl.ds(batch[b, d], 1), :]
         for b in range(count):
             picked[pl.ds(count + b, 1), :] = feat_wide[pl.ds(ids_smem[d, 0, b], 1), :]
         inputs_send[pl.ds(pl.multiple_of(d * both, both), both), :] = picked[pl.ds(0, both), :].astype(bf16)
@@ -198,17 +220,19 @@
     pick_feat(me)
     keep_inputs = keep(inputs_send, me, inputs, me, both, FEAT_IN)
     keep_inputs.start()
-    each(spread_hist, devices // 2, devices)
+    each(spread_hist, devices // 4, devices)
 
     keep_inputs.wait()
     wait_all(inputs, (devices - 1) * both, sems.at[1, FEAT_IN])
     load_inputs = functools.partial(load_part, inputs)
     load_inputs(0).start()
     load_inputs(1).start()
-    load_wide(load_inputs, 2)
+    for q in range(2):
+        load_inputs(q).wait()
+        spread(stage.at[q], wide, both, devices // 2, q * (devices // 2))
 
     def order_inputs(b, carry):
-        given[b] = wide[pl.ds(b, lanes, stride=both), :].astype(bf16)
+        given[b] = wide[pl.ds(b, lanes, stride=both + pad), :].astype(bf16)
         return carry
 
     lax.fori_loop(0, both, order_inputs, 0, unroll=2)
@@ -260,7 +284,7 @@
         dst[pl.ds(pl.multiple_of(d * height, height), height), :] = picked[...].astype(bf16)
 
     def pick_halo(d):
-        pick_wide(halo_send, d, lambda b: ids_smem[d, 0, lanes // 2 + b])
+        pick_wide(halo_send, d, lambda b: ids_smem[d, 0, 64 + b])
 
     def serve_halo(d):
         pick_halo(d)
@@ -280,7 +304,7 @@
     load_wide(load_push, 4)
 
     def pick_push(o):
-        pick_wide(wide_send, o, lambda p: inverse[o, p])
+        pick_wide(wide_send, o, lambda p: ids_smem[o, 0, 128 + p])
 
     def serve_push(o):
         pick_push(o)
@@ -345,7 +369,7 @@
     wait_all(pushed, (devices - 1) * height, sems.at[0, PUSH_IN])
 
 
-def run_step(batch, inverse, near, ids, features, history, tiles, w_in, w_layers):
+def run_step(batch, own, near, halo, pull, features, history, tiles, w_in, w_layers):
     anywhere = pl.BlockSpec(memory_space=pl.ANY)
     smem = pl.BlockSpec(memory_space=pltpu.SMEM)
     vmem = pl.BlockSpec(memory_space=pltpu.VMEM)
@@ -353,13 +377,16 @@
     sliced = shape(4 * rows, lanes)
     return pl.pallas_call(
         step_body,
-        in_specs=[smem, smem, smem, vmem, vmem, anywhere, anywhere, vmem, vmem],
+        in_specs=[anywhere, smem, smem, smem, smem, vmem, anywhere, anywhere, vmem, vmem],
         out_specs=[anywhere] * 6,
         out_shape=[shape(rows, 4 * lanes), shape(2 * rows, lanes), sliced, sliced, sliced, sliced],
         scratch_shapes=[
-            pltpu.VMEM((devices, 1, lanes), jnp.int32),
-            pltpu.SMEM((devices, 1, lanes), jnp.int32),
-            pltpu.VMEM((rows, lanes), f32),
+            pltpu.SMEM((count, devices), jnp.int32),
+            pltpu.SMEM((1, 2 * lanes), jnp.int32),
+            pltpu.VMEM((1, 2 * lanes), jnp.int32),
+            pltpu.VMEM((devices, 1, 2 * lanes), jnp.int32),
+            pltpu.SMEM((devices, 1, 2 * lanes), jnp.int32),
+            pltpu.VMEM((count * (lanes + pad), lanes), f32),
             pltpu.VMEM((4 * rows, lanes), f32),
             pltpu.VMEM((2, rows, lanes), bf16),
             pltpu.VMEM((rows, lanes), bf16),
@@ -376,25 +403,27 @@
             pltpu.SemaphoreType.DMA((2, WAYS)),
             pltpu.SemaphoreType.DMA((WAYS,)),
             pltpu.SemaphoreType.DMA((2,)),
-            pltpu.SemaphoreType.DMA((1,)),
+            pltpu.SemaphoreType.DMA((2,)),
             pltpu.SemaphoreType.DMA((2,)),
         ],
         compiler_params=pltpu.CompilerParams(
             vmem_limit_bytes=vmem_bytes, collective_id=1, has_side_effects=True
         ),
         cost_estimate=pl.CostEstimate(flops=14_000_000_000, bytes_accessed=100_000_000, transcendentals=0),
-    )(batch, inverse, near, ids, features, history, tiles, w_in, w_layers)
+    )(batch, own, near, halo, pull, features, history, tiles, w_in, w_layers)
 
 
 def place_body(pushed, second, fresh, result, wide):
     result[...] = second[...]
-    widen(pushed, wide, 0, rows)
+    spread(pushed, wide, height, 32)
 
     def move(a, carry):
-        fresh[pl.ds(pl.multiple_of(a * 32, 32), 32), :] = wide[pl.ds(a, 32, stride=height), :].astype(bf16)
-        return carry
-
-    lax.fori_loop(0, height, move, 0, unroll=4)
+        fresh[pl.ds(pl.multiple_of(a * 32, 32), 32), :] = wide[
+            pl.ds(a, 32, stride=height + pad), :
+        ].astype(bf16)
+        return carry
+
+    lax.fori_loop(0, height, move, 0, unroll=8)
 
 
 def place(pushed, second):
@@ -406,38 +435,22 @@
         in_specs=[pl.BlockSpec((rows, lanes), lambda q: (q, 0)), quarter],
         out_specs=[pl.BlockSpec((rows, lanes), lambda q: (0, q)), quarter],
         out_shape=[full, full],
-        scratch_shapes=[pltpu.VMEM((rows, lanes), f32)],
+        scratch_shapes=[pltpu.VMEM((32 * (height + pad), lanes), f32)],
         compiler_params=pltpu.CompilerParams(vmem_limit_bytes=vmem_bytes),
         cost_estimate=pl.CostEstimate(flops=0, bytes_accessed=40_000_000, transcendentals=0),
     )(pushed, second)
 
 
-def invert(batch):
-    flat = batch.reshape(-1)
-    spot = jnp.arange(flat.shape[0], dtype=jnp.int32)
-    owner = (flat // count)[:, None] == jnp.arange(devices, dtype=jnp.int32)[None, :]
-    place = (flat % count)[:, None] == jnp.arange(count, dtype=jnp.int32)[None, :]
-    low = jnp.where(place, (spot % 64)[:, None], 0).astype(bf16)
-    high = jnp.where(place, (spot // 64)[:, None], 0).astype(bf16)
-    found = lax.dot_general(
-        owner.astype(bf16),
-        jnp.concatenate([low, high], axis=1),
-        (((0,), (0,)), ((), ())),
-        preferred_element_type=f32,
-    ).astype(jnp.int32)
-    return found[:, :count] + 64 * found[:, count:]
+def own_places(batch):
+    spot = jnp.arange(batch.size, dtype=jnp.int32).reshape(batch.shape)[:, :, None]
+    cluster = lax.axis_index("dev") * count + jnp.arange(count, dtype=jnp.int32)
+    return jnp.sum(jnp.where(batch[:, :, None] == cluster, spot, 0), axis=(0, 1)).reshape(1, count)
 
 
 def local(features, history, batch_clusters, pull_list, halo_ref, in_ref, tiles, w_in, w_layers):
-    owner = halo_ref.reshape(count)
-    slots = jnp.arange(devices, dtype=jnp.int32)
-    spot = jnp.sum(
-        jnp.where(owner[:, None] == slots[None, :], pull_list.reshape(1, devices), 0), axis=1
-    )
-    mine = jnp.pad(owner * count + spot, (0, lanes // 2 - count))
-    mine = jnp.concatenate([mine, 4 * mine]).reshape(1, lanes)
     second, _, _, _, _, pushed = run_step(
-        batch_clusters, 4 * invert(batch_clusters), in_ref, mine, features, history, tiles, w_in, w_layers
+        batch_clusters.T, own_places(batch_clusters), in_ref, halo_ref, pull_list,
+        features, history, tiles, w_in, w_layers,
     )
     fresh, second_layer = place(pushed, second)
     return (second_layer, fresh)

time: 407 us -> 397 us (0.975)
  the two profiles are of different devices: /device:TPU:1 before, /device:TPU:69 now
where the time goes in v4:
time: 397 us
  Pallas kernels  394 us (99%)
    pallas_call x1, Pallas kernels, run_step(): pl.pallas_call(step_body, in_specs=[anywhere, smem, smem, smem, smem, vme...  384 us
    pallas_call x1, Pallas kernels, place(): pl.pallas_call(place_body, grid=(4,), in_specs=[pl.BlockSpec((rows, lanes...  10.8 us

profile of v4, /device:TPU:69, one launch (start us, length us, event | category | flops | bytes accessed | tf_op | source)
XLA Modules:
  0.0 396.7 jit_solution(18150242220807353449)
XLA Ops:
  0.7 1.6 select_reduce_fusion
  2.2 383.7 %shard_map.104 = (bf16[6144,512]{1,0:T(8,128)(2,1)}, bf16[12288,128]{1,0:T(8,128)(2,1)}, bf16[24576,128]{1,0:T(8,128)(2,1)}, bf16[24576,128]{1,0:T(8,128)(2,1)},...) custom-call(s32[48,128]{1,0:T(8,128)} %bitcast.2, s32[1,48]{1,0:T(1,128)} %bitcast.3, s32[1,48]{1,0:T(1,128)} %near.1, ...), custom_call_target="tpu_custom_call" | custom-call | flops 14000000000 | bytes 100000000 | tf_op jit(solution)/shard_map/pallas_call | solution.py:378
  385.9 10.8 %shard_map.105 = (bf16[6144,512]{1,0:T(8,128)(2,1)}, bf16[6144,512]{1,0:T(8,128)(2,1)}) custom-call(bf16[24576,128]{1,0:T(8,128)(2,1)} %get-tuple-element.6.pushed, bf16[6144,512]{1,0:T(8,128)(2,1)} %get-tuple-element.7.second), custom_call_target="tpu_custom_call" | custom-call | bytes 40000000 | tf_op jit(solution)/shard_map/pallas_call | solution.py:432
  (2 shorter events, 0.0 us)

commit v5 on v4

--- a/solution.py
+++ b/solution.py
@@ -27,6 +27,8 @@
 IDS, FEAT_OUT, HIST_OUT, FEAT_IN, PUSH_OUT, HIST_IN, PUSH_IN = range(7)
 WAYS = 7
 
+turns = ((37, 91), (37, 91), (91, 37), (45, 83), (83, 45), (53, 75), (75, 53))
+
 
 def partner(me, k):
     z, x, y, core = me // 32, me // 8 % 4, me // 2 % 4, me % 2
@@ -35,8 +37,10 @@
     )
 
 
-def order(me, i):
-    return partner(me, i * (37 + 54 * (me % 2)) % devices)
+def order(me, i, way):
+    first, second = turns[way]
+    step = first + (second - first) * (me % 2)
+    return partner(me, i * step % devices)
 
 
 def at(ref, slot, size):
@@ -59,8 +63,8 @@
     ).start()
 
 
-def send_pieces(src_ref, src_slot, dst_ref, dst_slot, sems, way, peer):
-    for part in range(height // piece):
+def send_pieces(src_ref, src_slot, dst_ref, dst_slot, sems, way, peer, parts=range(height // piece)):
+    for part in parts:
         src = src_ref.at[pl.ds(pl.multiple_of(src_slot * height + part * piece, piece), piece)]
         dst = dst_ref.at[pl.ds(pl.multiple_of(dst_slot * height + part * piece, piece), piece)]
         send(src, dst, sems, way, peer)
@@ -129,9 +133,9 @@
     def keep(src, src_slot, dst, dst_slot, size, way):
         return pltpu.make_async_copy(at(src, src_slot, size), at(dst, dst_slot, size), local_sem.at[way])
 
-    def each(body, first, last):
+    def each(way, body, first, last):
         def step(i, carry):
-            body(order(me, i))
+            body(order(me, i, way))
             return carry
 
         lax.fori_loop(first, last, step, 0)
@@ -160,7 +164,7 @@
         pack_feat(m)
         send(at(feat_send, m, count), at(feat_mid, me, count), sems, FEAT_OUT, m)
 
-    each(spread_feat, 1, devices)
+    each(FEAT_OUT, spread_feat, 1, devices)
     pack_feat(me)
     keep_feat = keep(feat_send, me, feat_mid, me, count, FEAT_OUT)
     keep_feat.start()
@@ -174,7 +178,7 @@
     to_vmem = pltpu.make_async_copy(mine_smem, mine, local_sem.at[IDS])
     to_vmem.start()
     to_vmem.wait()
-    each(lambda m: send(mine, ids_mid.at[me], sems, IDS, m), 1, devices)
+    each(IDS, lambda m: send(mine, ids_mid.at[me], sems, IDS, m), 1, devices)
     keep_ids = pltpu.make_async_copy(mine, ids_mid.at[me], local_sem.at[IDS])
     keep_ids.start()
 
@@ -192,7 +196,7 @@
     pack_wide(me)
     keep_hist = keep(wide_send, me, hist_mid, me, height, HIST_OUT)
     keep_hist.start()
-    each(spread_hist, 1, devices // 4)
+    each(HIST_OUT, spread_hist, 1, devices // 4)
 
     load_batch.wait()
     keep_ids.wait()
@@ -216,11 +220,11 @@
         pick_feat(d)
         send(at(inputs_send, d, both), at(inputs, me, both), sems, FEAT_IN, d)
 
-    each(serve_feat, 1, devices)
+    each(FEAT_IN, serve_feat, 1, devices)
     pick_feat(me)
     keep_inputs = keep(inputs_send, me, inputs, me, both, FEAT_IN)
     keep_inputs.start()
-    each(spread_hist, devices // 4, devices)
+    each(HIST_OUT, spread_hist, devices // 4, devices)
 
     keep_inputs.wait()
     wait_all(inputs, (devices - 1) * both, sems.at[1, FEAT_IN])
@@ -265,9 +269,11 @@
 
     def spread_push(m):
         pack_wide(m)
-        send_pieces(wide_send, m, push_mid, me, sems, PUSH_OUT, m)
-
-    each(spread_push, 1, devices)
+        send_pieces(wide_send, m, push_mid, me, sems, PUSH_OUT, m, (0,))
+
+    each(PUSH_OUT, spread_push, 1, devices)
+    for part in range(1, height // piece):
+        each(PUSH_OUT, lambda m: send_pieces(wide_send, m, push_mid, me, sems, PUSH_OUT, m, (part,)), 1, devices)
     pack_wide(me)
     keep_push = keep(wide_send, me, push_mid, me, height, PUSH_OUT)
     keep_push.start()
@@ -288,9 +294,11 @@
 
     def serve_halo(d):
         pick_halo(d)
-        send_pieces(halo_send, d, halo, me, sems, HIST_IN, d)
-
-    each(serve_halo, 1, devices)
+        send_pieces(halo_send, d, halo, me, sems, HIST_IN, d, (0,))
+
+    each(HIST_IN, serve_halo, 1, devices)
+    for part in range(1, height // piece):
+        each(HIST_IN, lambda d: send_pieces(halo_send, d, halo, me, sems, HIST_IN, d, (part,)), 1, devices)
     pick_halo(me)
     keep_halo = keep(halo_send, me, halo, me, height, HIST_IN)
     keep_halo.start()
@@ -308,9 +316,11 @@
 
     def serve_push(o):
         pick_push(o)
-        send_pieces(wide_send, o, pushed, me, sems, PUSH_IN, o)
-
-    each(serve_push, 1, devices)
+        send_pieces(wide_send, o, pushed, me, sems, PUSH_IN, o, (0,))
+
+    each(PUSH_IN, serve_push, 1, devices)
+    for part in range(1, height // piece):
+        each(PUSH_IN, lambda o: send_pieces(wide_send, o, pushed, me, sems, PUSH_IN, o, (part,)), 1, devices)
     pick_push(me)
     keep_pushed = keep(wide_send, me, pushed, me, height, PUSH_IN)
     keep_pushed.start()

time: 397 us -> 367 us (0.924)
  the two profiles are of different devices: /device:TPU:69 before, /device:TPU:1 now
where the time goes in v5:
time: 367 us; the launch traced here: 364 us
  Pallas kernels  361 us (98%)
    pallas_call x1, Pallas kernels, run_step(): pl.pallas_call(step_body, in_specs=[anywhere, smem, smem, smem, smem, vme...  351 us
    pallas_call x1, Pallas kernels, place(): pl.pallas_call(place_body, grid=(4,), in_specs=[pl.BlockSpec((rows, lanes...  10.8 us

profile of v5, /device:TPU:1, one launch (start us, length us, event | category | flops | bytes accessed | tf_op | source)
XLA Modules:
  0.0 363.7 jit_solution(9237273589163230114)
XLA Ops:
  0.7 1.6 select_reduce_fusion
  2.2 350.7 %shard_map.104 = (bf16[6144,512]{1,0:T(8,128)(2,1)}, bf16[12288,128]{1,0:T(8,128)(2,1)}, bf16[24576,128]{1,0:T(8,128)(2,1)}, bf16[24576,128]{1,0:T(8,128)(2,1)},...) custom-call(s32[48,128]{1,0:T(8,128)} %bitcast.2, s32[1,48]{1,0:T(1,128)} %bitcast.3, s32[1,48]{1,0:T(1,128)} %near.1, ...), custom_call_target="tpu_custom_call" | custom-call | flops 14000000000 | bytes 100000000 | tf_op jit(solution)/shard_map/pallas_call | solution.py:388
  352.9 10.8 %shard_map.105 = (bf16[6144,512]{1,0:T(8,128)(2,1)}, bf16[6144,512]{1,0:T(8,128)(2,1)}) custom-call(bf16[24576,128]{1,0:T(8,128)(2,1)} %get-tuple-element.6.pushed, bf16[6144,512]{1,0:T(8,128)(2,1)} %get-tuple-element.7.second), custom_call_target="tpu_custom_call" | custom-call | bytes 40000000 | tf_op jit(solution)/shard_map/pallas_call | solution.py:442
  (2 shorter events, 0.0 us)

commit v6 on v5

--- a/solution.py
+++ b/solution.py
@@ -152,23 +152,6 @@
     load_history(0).start()
     load_history(1).start()
     load_batch.start()
-    spread(feat_ref, feat_wide, lanes, count)
-    pl.semaphore_wait(barrier, devices - 1)
-
-    def pack_feat(m):
-        feat_send[pl.ds(pl.multiple_of(m * count, count), count), :] = feat_wide[
-            pl.ds(m, count, stride=lanes + pad), :
-        ].astype(bf16)
-
-    def spread_feat(m):
-        pack_feat(m)
-        send(at(feat_send, m, count), at(feat_mid, me, count), sems, FEAT_OUT, m)
-
-    each(FEAT_OUT, spread_feat, 1, devices)
-    pack_feat(me)
-    keep_feat = keep(feat_send, me, feat_mid, me, count, FEAT_OUT)
-    keep_feat.start()
-
     for b in range(count):
         slot = halo_ref[0, b]
         cluster = slot * count + pull_ref[0, slot]
@@ -177,10 +160,22 @@
         mine_smem[0, 128 + b] = 4 * own_ref[0, b]
     to_vmem = pltpu.make_async_copy(mine_smem, mine, local_sem.at[IDS])
     to_vmem.start()
-    to_vmem.wait()
-    each(IDS, lambda m: send(mine, ids_mid.at[me], sems, IDS, m), 1, devices)
-    keep_ids = pltpu.make_async_copy(mine, ids_mid.at[me], local_sem.at[IDS])
-    keep_ids.start()
+    spread(feat_ref, feat_wide, lanes, count)
+    pl.semaphore_wait(barrier, devices - 1)
+
+    def pack_feat(m):
+        feat_send[pl.ds(pl.multiple_of(m * count, count), count), :] = feat_wide[
+            pl.ds(m, count, stride=lanes + pad), :
+        ].astype(bf16)
+
+    def spread_feat(m):
+        pack_feat(m)
+        send(at(feat_send, m, count), at(feat_mid, me, count), sems, FEAT_OUT, m)
+
+    each(FEAT_OUT, spread_feat, 1, devices)
+    pack_feat(me)
+    keep_feat = keep(feat_send, me, feat_mid, me, count, FEAT_OUT)
+    keep_feat.start()
 
     def pack_wide(m):
         wide_send[pl.ds(pl.multiple_of(m * height, height), height), :] = wide[
@@ -189,14 +184,24 @@
 
     def spread_hist(m):
         pack_wide(m)
-        send_pieces(wide_send, m, hist_mid, me, sems, HIST_OUT, m)
+        send_pieces(wide_send, m, hist_mid, me, sems, HIST_OUT, m, (0,))
+
+    def spread_rest(first, last):
+        for part in range(1, height // piece):
+            each(HIST_OUT, lambda m: send_pieces(wide_send, m, hist_mid, me, sems, HIST_OUT, m, (part,)), first, last)
 
     load_wide(load_history, 4)
     load_tiles.start()
     pack_wide(me)
     keep_hist = keep(wide_send, me, hist_mid, me, height, HIST_OUT)
     keep_hist.start()
-    each(HIST_OUT, spread_hist, 1, devices // 4)
+    each(HIST_OUT, spread_hist, 1, 8)
+    to_vmem.wait()
+    each(IDS, lambda m: send(mine, ids_mid.at[me], sems, IDS, m), 1, devices)
+    keep_ids = pltpu.make_async_copy(mine, ids_mid.at[me], local_sem.at[IDS])
+    keep_ids.start()
+    each(HIST_OUT, spread_hist, 8, devices // 4)
+    spread_rest(1, devices // 4)
 
     load_batch.wait()
     keep_ids.wait()
@@ -225,6 +230,7 @@
     keep_inputs = keep(inputs_send, me, inputs, me, both, FEAT_IN)
     keep_inputs.start()
     each(HIST_OUT, spread_hist, devices // 4, devices)
+    spread_rest(devices // 4, devices)
 
     keep_inputs.wait()
     wait_all(inputs, (devices - 1) * both, sems.at[1, FEAT_IN])

time: 367 us -> 361 us (0.984)
  Pallas kernels: 361 us -> 357 us
    pallas_call x1, Pallas kernels: 351 us -> 346 us  [run_step(): pl.pallas_call(step_body, in_specs=[anywhere, smem, smem, smem, smem, vme...]
where the time goes in v6:
time: 361 us; the launch traced here: 359 us
  Pallas kernels  357 us (99%)
    pallas_call x1, Pallas kernels, run_step(): pl.pallas_call(step_body, in_specs=[anywhere, smem, smem, smem, smem, vme...  346 us
    pallas_call x1, Pallas kernels, place(): pl.pallas_call(place_body, grid=(4,), in_specs=[pl.BlockSpec((rows, lanes...  10.8 us

profile of v6, /device:TPU:1, one launch (start us, length us, event | category | flops | bytes accessed | tf_op | source)
XLA Modules:
  0.0 359.2 jit_solution(9355595928351208975)
XLA Ops:
  0.7 1.6 select_reduce_fusion
  2.2 346.2 %shard_map.104 = (bf16[6144,512]{1,0:T(8,128)(2,1)}, bf16[12288,128]{1,0:T(8,128)(2,1)}, bf16[24576,128]{1,0:T(8,128)(2,1)}, bf16[24576,128]{1,0:T(8,128)(2,1)},...) custom-call(s32[48,128]{1,0:T(8,128)} %bitcast.2, s32[1,48]{1,0:T(1,128)} %bitcast.3, s32[1,48]{1,0:T(1,128)} %near.1, ...), custom_call_target="tpu_custom_call" | custom-call | flops 14000000000 | bytes 100000000 | tf_op jit(solution)/shard_map/pallas_call | solution.py:394
  348.4 10.8 %shard_map.105 = (bf16[6144,512]{1,0:T(8,128)(2,1)}, bf16[6144,512]{1,0:T(8,128)(2,1)}) custom-call(bf16[24576,128]{1,0:T(8,128)(2,1)} %get-tuple-element.6.pushed, bf16[6144,512]{1,0:T(8,128)(2,1)} %get-tuple-element.7.second), custom_call_target="tpu_custom_call" | custom-call | bytes 40000000 | tf_op jit(solution)/shard_map/pallas_call | solution.py:448
  (2 shorter events, 0.0 us)

commit v7 on v6

--- a/solution.py
+++ b/solution.py
@@ -402,8 +402,8 @@
             pltpu.VMEM((1, 2 * lanes), jnp.int32),
             pltpu.VMEM((devices, 1, 2 * lanes), jnp.int32),
             pltpu.SMEM((devices, 1, 2 * lanes), jnp.int32),
-            pltpu.VMEM((count * (lanes + pad), lanes), f32),
-            pltpu.VMEM((4 * rows, lanes), f32),
+            pltpu.VMEM(((count + 1) * (lanes + pad), lanes), f32),
+            pltpu.VMEM((4 * rows + 2 * lanes, lanes), f32),
             pltpu.VMEM((2, rows, lanes), bf16),
             pltpu.VMEM((rows, lanes), bf16),
             pltpu.VMEM((rows, lanes), bf16),
@@ -451,7 +451,7 @@
         in_specs=[pl.BlockSpec((rows, lanes), lambda q: (q, 0)), quarter],
         out_specs=[pl.BlockSpec((rows, lanes), lambda q: (0, q)), quarter],
         out_shape=[full, full],
-        scratch_shapes=[pltpu.VMEM((32 * (height + pad), lanes), f32)],
+        scratch_shapes=[pltpu.VMEM((33 * (height + pad), lanes), f32)],
         compiler_params=pltpu.CompilerParams(vmem_limit_bytes=vmem_bytes),
         cost_estimate=pl.CostEstimate(flops=0, bytes_accessed=40_000_000, transcendentals=0),
     )(pushed, second)

time: 361 us -> 361 us (level)
  no operation moved by 1% of the time
where the time goes in v7:
time: 361 us; the launch traced here: 359 us
  Pallas kernels  357 us (99%)
    pallas_call x1, Pallas kernels, run_step(): pl.pallas_call(step_body, in_specs=[anywhere, smem, smem, smem, smem, vme...  346 us
    pallas_call x1, Pallas kernels, place(): pl.pallas_call(place_body, grid=(4,), in_specs=[pl.BlockSpec((rows, lanes...  10.8 us

profile of v7, /device:TPU:1, one launch (start us, length us, event | category | flops | bytes accessed | tf_op | source)
XLA Modules:
  0.0 359.2 jit_solution(1603715230436360043)
XLA Ops:
  0.7 1.6 select_reduce_fusion
  2.2 346.2 %shard_map.104 = (bf16[6144,512]{1,0:T(8,128)(2,1)}, bf16[12288,128]{1,0:T(8,128)(2,1)}, bf16[24576,128]{1,0:T(8,128)(2,1)}, bf16[24576,128]{1,0:T(8,128)(2,1)},...) custom-call(s32[48,128]{1,0:T(8,128)} %bitcast.2, s32[1,48]{1,0:T(1,128)} %bitcast.3, s32[1,48]{1,0:T(1,128)} %near.1, ...), custom_call_target="tpu_custom_call" | custom-call | flops 14000000000 | bytes 100000000 | tf_op jit(solution)/shard_map/pallas_call | solution.py:394
  348.4 10.8 %shard_map.105 = (bf16[6144,512]{1,0:T(8,128)(2,1)}, bf16[6144,512]{1,0:T(8,128)(2,1)}) custom-call(bf16[24576,128]{1,0:T(8,128)(2,1)} %get-tuple-element.6.pushed, bf16[6144,512]{1,0:T(8,128)(2,1)} %get-tuple-element.7.second), custom_call_target="tpu_custom_call" | custom-call | bytes 40000000 | tf_op jit(solution)/shard_map/pallas_call | solution.py:448
  (2 shorter events, 0.0 us)
